TPU v7x, 256 devices: a whole 4x4x8 slice. The times are simulated.
256 devices in a mesh: cols: 64 (over x_hi, z, y), rows: 4 (over x_lo, core).
Axes of the slice: x: 4 (x_hi: 2, x_lo: 2; x = x_hi * 2 + x_lo), y: 4, z: 8, core: 2. Of those that a mesh axis runs over, the one named last changes fastest.
Arguments:
- gradient: bfloat16 [8192, 28672], P('rows', 'cols'), may hold values from -6 to 6
- eigenbasis: float32 [8192, 8192], P('rows', 'cols'), may hold values from -0.0625 to 0.0625
- first_moment: float32 [4, 256, 28672], P(None, 'rows', 'cols'), may hold values from -4 to 4
- second_moment: float32 [4, 256, 28672], P(None, 'rows', 'cols'), may hold values from 0.2 to 2
- prior_update: float32 [8192, 28672], P('rows', 'cols'), may hold values from -3 to 3
- group_ids: int32 [4], replicated, may hold values from 0 to 31, as said below
Outputs:
- first_out: float32 [4, 256, 28672], P(None, 'rows', 'cols')
- second_out: float32 [4, 256, 28672], P(None, 'rows', 'cols')
- update: float32 [8192, 28672], P('rows', 'cols')
Inputs may be any that keep to these rules, and one draw needn't show every extreme that they name: `group_ids`: the 4 entries are distinct.
All inputs are finite; a program needn't handle non-finite values.
Results may differ from a plain program's by a relative error of at most 0.0003.
Values sent between devices are 32-bit elements; how exact they have to be, the bound alone decides.
A program may use at most 64 MiB of HBM per device.

v0:
```python
import jax.numpy as jnp
from jax import lax

GROUP = 256
GROUPS = 4


beta_one = 0.9


beta_two = 0.95


correct_one = 1.0 - 0.9**10


correct_two = 1.0 - 0.95**10


epsilon = 1e-08


def reference(gradient, eigenbasis, first_moment, second_moment, prior_update, group_ids):
    grad_float = gradient.astype(jnp.float32)
    update = prior_update
    firsts = []
    seconds = []
    for group_slot in range(GROUPS):
        begin = (group_ids[group_slot] * GROUP).astype(jnp.int32)
        group_basis = lax.dynamic_slice_in_dim(eigenbasis, begin, GROUP, 1)
        rotated = jnp.dot(
            group_basis.T,
            grad_float,
            precision=lax.Precision.HIGHEST,
            preferred_element_type=jnp.float32,
        )
        moment_one = beta_one * first_moment[group_slot] + (1.0 - beta_one) * rotated
        moment_two = beta_two * second_moment[group_slot] + (1.0 - beta_two) * rotated * rotated
        adjusted = moment_one / correct_one / (jnp.sqrt(moment_two / correct_two) + epsilon)
        update = update + jnp.dot(
            group_basis,
            adjusted,
            precision=lax.Precision.HIGHEST,
            preferred_element_type=jnp.float32,
        )
        firsts.append(moment_one)
        seconds.append(moment_two)
    return (jnp.stack(firsts), jnp.stack(seconds), update)


def solution(mesh):
    return reference
```

profile of v0, /device:TPU:1, one launch (start us, length us, event | category | flops | bytes accessed | tf_op | source)
XLA Modules:
  0.0 675.6 jit_solution(6362717362235273123)
XLA Ops:
  7.2 0.0 copy-start
  7.2 0.0 copy-start.9
  7.2 15.3 %all-to-all-start = ((f32[1,64,32,128]{3,2,0,1:T(8,128)}), f32[1,64,32,128]{3,2,0,1:T(8,128)S(1)}, u32[]{:S(2)}, u32[]{:S(2)}) async-start(f32[1,64,32,128]{3,2,0,1:T(8,128)} %bitcast.95), calls=%async_computation | async-start | bytes 2097152 | tf_op jit(solution)/call_exported
  22.5 0.0 all-gather.23.cloned.1.call-start
  22.5 0.0 copy-done.9
  22.5 0.7 fusion.12
  25.8 24.9 %all-to-all-done = f32[1,64,32,128]{3,2,0,1:T(8,128)S(1)} async-done(((f32[1,64,32,128]{3,2,0,1:T(8,128)}), f32[1,64,32,128]{3,2,0,1:T(8,128)S(1)}, u32[]{:S(2)}, u32[]{:S(2)}) %all-to-all-start) | async-done | bytes 1048608 | tf_op jit(solution)/call_exported
  50.7 0.6 copy.1
  51.3 0.6 copy.4
  51.9 0.7 constant_dynamic-slice_fusion.3
  52.6 0.0 all-gather.23.cloned.1.call-update
  52.6 0.0 all-gather.17.cloned.1.call-start
  52.7 0.7 all-gather.17.cloned.1.call-update
  53.4 0.0 all-gather.19.cloned.1.call-start
  53.4 0.7 all-gather.19.cloned.1.call-update
  54.1 0.0 all-gather.21.cloned.1.call-start
  54.2 0.5 all-gather.21.cloned.1.call-update
  54.7 0.0 reduce-scatter.19.cloned.1.call-start
  54.7 110.1 %all-gather.23.cloned.1.call-done = f32[2048,256]{1,0:T(8,128)} async-done(((f32[32,256]{1,0:T(8,128)}), f32[2048,256]{1,0:T(8,128)}) %all-gather.23.cloned.1.call-update) | async-done | bytes 2097168 | tf_op jit(solution)/dynamic_slice | solution.py:30
  164.8 0.0 copy-done
  164.9 5.8 fusion.16
  170.7 0.0 reduce-scatter.19.cloned.1.call-update
  170.7 0.0 reduce-scatter.13.cloned.1.call-start
  170.7 113.8 %all-gather.17.cloned.1.call-done = f32[2048,256]{1,0:T(8,128)} async-done(((f32[32,256]{1,0:T(8,128)}), f32[2048,256]{1,0:T(8,128)}) %all-gather.17.cloned.1.call-update) | async-done | bytes 2097168 | tf_op jit(solution)/dynamic_slice | solution.py:30
  284.5 5.9 fusion.13
  290.4 0.0 reduce-scatter.13.cloned.1.call-update
  290.4 0.2 reduce-scatter.15.cloned.1.call-start
  290.6 113.5 %all-gather.19.cloned.1.call-done = f32[2048,256]{1,0:T(8,128)} async-done(((f32[32,256]{1,0:T(8,128)}), f32[2048,256]{1,0:T(8,128)}) %all-gather.19.cloned.1.call-update) | async-done | bytes 2097168 | tf_op jit(solution)/dynamic_slice | solution.py:30
  404.2 5.8 fusion.14
  410.0 0.0 reduce-scatter.15.cloned.1.call-update
  410.0 0.0 copy-start.6
  410.0 0.0 copy-start.8
  410.0 0.0 reduce-scatter.17.cloned.1.call-start
  410.1 113.0 %all-gather.21.cloned.1.call-done = f32[2048,256]{1,0:T(8,128)} async-done(((f32[32,256]{1,0:T(8,128)}), f32[2048,256]{1,0:T(8,128)}) %all-gather.21.cloned.1.call-update) | async-done | bytes 2097168 | tf_op jit(solution)/dynamic_slice | solution.py:30
  523.1 5.8 fusion.15
  528.9 0.0 reduce-scatter.17.cloned.1.call-update
  528.9 18.3 %reduce-scatter.19.cloned.1.call-done = f32[64,448]{1,0:T(8,128)} async-done(((f32[256,448]{1,0:T(8,128)}), f32[64,448]{1,0:T(8,128)}) %reduce-scatter.19.cloned.1.call-update) | async-done | bytes 114704
  547.3 0.0 copy-start.7
  547.3 24.0 %reduce-scatter.13.cloned.1.call-done = f32[64,448]{1,0:T(8,128)} async-done(((f32[256,448]{1,0:T(8,128)}), f32[64,448]{1,0:T(8,128)}) %reduce-scatter.13.cloned.1.call-update) | async-done | bytes 114704
  571.2 24.7 %reduce-scatter.15.cloned.1.call-done = f32[64,448]{1,0:T(8,128)} async-done(((f32[256,448]{1,0:T(8,128)}), f32[64,448]{1,0:T(8,128)}) %reduce-scatter.15.cloned.1.call-update) | async-done | bytes 114704
  595.9 24.7 %reduce-scatter.17.cloned.1.call-done = f32[64,448]{1,0:T(8,128)} async-done(((f32[256,448]{1,0:T(8,128)}), f32[64,448]{1,0:T(8,128)}) %reduce-scatter.17.cloned.1.call-update) | async-done | bytes 114704
  620.6 0.0 copy-done.6
  620.6 0.0 copy-done.8
  620.6 1.4 add_divide_fusion
  622.1 7.3 %all-gather.5 = f32[256,448]{1,0:T(8,128)S(1)} all-gather(f32[64,448]{1,0:T(8,128)S(1)} %get-tuple-element.3), channel_id=15, replica_groups=[64,4]<=[256], dimensions={0}, use_global_device_ids=true | all-gather | bytes 573440 | tf_op jit(solution)/div | solution.py:39
  629.4 0.0 copy-start.2
  629.4 7.4 %all-gather.7 = f32[256,448]{1,0:T(8,128)S(1)} all-gather(f32[64,448]{1,0:T(8,128)S(1)} %get-tuple-element.2), channel_id=17, replica_groups=[64,4]<=[256], dimensions={0}, use_global_device_ids=true | all-gather | bytes 573440 | tf_op jit(solution)/div | solution.py:39
  636.8 7.3 %all-gather.9 = f32[256,448]{1,0:T(8,128)S(1)} all-gather(f32[64,448]{1,0:T(8,128)S(1)} %get-tuple-element.1), channel_id=19, replica_groups=[64,4]<=[256], dimensions={0}, use_global_device_ids=true | all-gather | bytes 573440 | tf_op jit(solution)/div | solution.py:39
  644.1 7.5 %all-gather.11 = f32[256,448]{1,0:T(8,128)S(1)} all-gather(f32[64,448]{1,0:T(8,128)S(1)} %get-tuple-element), channel_id=21, replica_groups=[64,4]<=[256], dimensions={0}, use_global_device_ids=true | all-gather | bytes 573440 | tf_op jit(solution)/div | solution.py:39
  651.6 0.0 copy-done.7
  651.6 1.1 pad_maximum_fusion
  652.7 0.0 copy-done.2
  652.7 0.0 copy-start.3
  652.7 3.3 fusion.17
  656.0 0.0 copy-done.3
  656.0 0.0 copy-start.4
  656.0 3.3 fusion.18
  659.4 0.0 copy-done.4
  659.4 0.0 copy-start.1
  659.4 0.0 copy-start.5
  659.4 3.3 fusion.19
  662.7 0.0 copy-done.1
  662.7 0.0 copy-done.5
  662.8 6.0 add_add_fusion
  (1 shorter events, 0.0 us)
Async XLA Ops:
  7.2 157.7 %copy-start = (bf16[2048,448]{0,1:T(8,128)(2,1)S(1)}, bf16[2048,448]{0,1:T(8,128)(2,1)}, u32[]{:S(2)}) copy-start(bf16[2048,448]{0,1:T(8,128)(2,1)} %param.3) | copy-start | bytes 5505028
  7.2 15.3 %copy-start.9 = (s32[4]{0:T(128)S(1)}, s32[4]{0:T(128)}, u32[]{:S(2)}) copy-start(s32[4]{0:T(128)} %param.2) | copy-start | bytes 52
  7.2 43.5 %all-to-all-start = ((f32[1,64,32,128]{3,2,0,1:T(8,128)}), f32[1,64,32,128]{3,2,0,1:T(8,128)S(1)}, u32[]{:S(2)}, u32[]{:S(2)}) async-start(f32[1,64,32,128]{3,2,0,1:T(8,128)} %bitcast.95), calls=%async_computation | async-start | bytes 2097152 | tf_op jit(solution)/call_exported
  22.5 142.4 %all-gather.23.cloned.1.call-start = ((), (), s32[]{:S(2)}) async-start(), calls=%async_computation.8 | async-start | bytes 2129920 | tf_op jit(solution)/dynamic_slice | solution.py:30
  52.6 231.9 %all-gather.17.cloned.1.call-start = ((), (), s32[]{:S(2)}) async-start(), calls=%async_computation.5 | async-start | bytes 2129920 | tf_op jit(solution)/dynamic_slice | solution.py:30
  53.4 350.8 %all-gather.19.cloned.1.call-start = ((), (), s32[]{:S(2)}) async-start(), calls=%async_computation.6 | async-start | bytes 2129920 | tf_op jit(solution)/dynamic_slice | solution.py:30
  54.1 469.0 %all-gather.21.cloned.1.call-start = ((), (), s32[]{:S(2)}) async-start(), calls=%async_computation.7 | async-start | bytes 2129920 | tf_op jit(solution)/dynamic_slice | solution.py:30
  54.7 492.6 %reduce-scatter.19.cloned.1.call-start = ((), (), s32[]{:S(2)}) async-start(), calls=%async_computation.12 | async-start | bytes 655360
  170.7 400.6 %reduce-scatter.13.cloned.1.call-start = ((), (), s32[]{:S(2)}) async-start(), calls=%async_computation.9 | async-start | bytes 655360
  290.4 305.5 %reduce-scatter.15.cloned.1.call-start = ((), (), s32[]{:S(2)}) async-start(), calls=%async_computation.10 | async-start | bytes 655360
  410.0 210.7 %copy-start.6 = (f32[4,64,448]{2,1,0:T(8,128)S(1)}, f32[4,64,448]{2,1,0:T(8,128)}, u32[]{:S(2)}) copy-start(f32[4,64,448]{2,1,0:T(8,128)} %param) | copy-start | bytes 1376260
  410.0 210.6 %copy-start.8 = (f32[4,64,448]{2,1,0:T(8,128)S(1)}, f32[4,64,448]{2,1,0:T(8,128)}, u32[]{:S(2)}) copy-start(f32[4,64,448]{2,1,0:T(8,128)} %param.4) | copy-start | bytes 1376260
  410.0 210.6 %reduce-scatter.17.cloned.1.call-start = ((), (), s32[]{:S(2)}) async-start(), calls=%async_computation.11 | async-start | bytes 655360
  547.3 104.3 %copy-start.7 = (f32[64,448]{1,0:T(8,128)S(1)}, f32[64,448]{1,0:T(8,128)}, u32[]{:S(2)}) copy-start(f32[64,448]{1,0:T(8,128)} %reduce-scatter.19.cloned.1.call-done) | copy-start | bytes 344068
  629.4 23.3 %copy-start.2 = (f32[2048,256]{1,0:T(8,128)S(1)}, f32[2048,256]{1,0:T(8,128)}, u32[]{:S(2)}) copy-start(f32[2048,256]{1,0:T(8,128)} %all-gather.17.cloned.1.call-done) | copy-start | bytes 6291460
  652.7 3.3 copy-start.3
  656.0 3.3 copy-start.4
  659.4 3.4 copy-start.1
  659.4 3.4 copy-start.5
Sparse Core Ops, SparseCore 0:
  52.8 112.0 all-gather.22
  169.0 115.4 all-gather.16
  288.7 115.4 all-gather.18
  407.6 115.4 all-gather.20
  526.0 21.1 reduce-scatter.18
  549.6 21.5 reduce-scatter.12
  574.3 21.5 reduce-scatter.14
  599.0 21.5 reduce-scatter.16
where the time goes:
time: 676 us
  waiting for transfers between devices  569 us (84%)
  matrix products  39.3 us (6%)
  blocking collectives  29.5 us (4%)
  between operations  16.9 us (2%)
  starting transfers between devices  15.8 us (2%)
    dynamic_slice x4, waiting for transfers between devices, reference(): group_basis = lax.dynamic_slice_in_dim(eigenbasis, begin, GROUP, 1)  450 us
    unnamed x12, waiting for transfers between devices  93.7 us
    div x4, blocking collectives, reference(): moment_one / correct_one / (jnp.sqrt(moment_two / correct_two) + epsilon)  29.5 us
    another operation x1, waiting for transfers between devices  24.9 us
    dot_general x4, matrix products, reference(): jnp.dot(group_basis.T, grad_float, precision=lax.Precision.HIGHEST, prefe...  23.3 us
    dot_general x4, matrix products, reference(): jnp.dot(group_basis, adjusted, precision=lax.Precision.HIGHEST, preferred...  16 us
    another operation x1, starting transfers between devices  15.3 us
  transfers between devices with their start and end apart: 9, of which 9 were waited for; matrix products, arithmetic and copies ran while one was open for 4% of the time, Pallas kernels for 0%

commit v1 on v0

v1 whole, which is shorter than its diff:
```python
import functools

import jax
import jax.numpy as jnp
from jax import lax
from jax.experimental import pallas as pl
from jax.experimental.pallas import tpu as pltpu
from jax.sharding import PartitionSpec as P

MESH = pl.DeviceIdType.MESH

GROUPS = 4
NX, NZ, NY = 2, 8, 4
PIECE = 32
GROUP = 256
QUARTER = 64
COLS = 448
ROWS = 2048
SPLIT = (16, 24)

beta_one = 0.9
beta_two = 0.95
correct_one = 1.0 - 0.9**10
correct_two = 1.0 - 0.95**10
epsilon = 1e-08

Z_MSGS = 7
Y_MSGS = 3
Z_TICKS = (0, 1, 2, 3, 4, 5, 6)
Y_BIG_TICKS = (0, 1, 4)
Y_SMALL_TICKS = (0, 1, 2)
TICKS = 8

SEM_X = 0
SEM_A1 = 1
SEM_B1 = SEM_A1 + 2 * Z_MSGS
SEM_A2 = SEM_B1 + 2 * Y_MSGS
SEM_B2 = SEM_A2 + 2 * Y_MSGS
SEM_RS1 = SEM_B2 + 2 * Z_MSGS
SEM_RS2 = SEM_RS1 + 1
SEM_AX = SEM_RS2 + 1
SEM_AC = SEM_AX + 1
SEM_AF = SEM_AC + 1
SEMS = SEM_AF + 1


def split_terms(value):
    high = value.astype(jnp.bfloat16)
    low = (value - high.astype(jnp.float32)).astype(jnp.bfloat16)
    return high, low


def kernel(ids, pieces, first_in, second_in, grad_hbm, prior_hbm,
           first_out, second_out, update_hbm,
           buf, grad, update, partial, rs1, xsend, rs2, adjusted,
           send_sem, recv_sem, local_sem, out_sem):
    cols = lax.axis_index("cols")
    rows = lax.axis_index("rows")
    xh = cols // (NZ * NY)
    z = (cols // NY) % NZ
    y = cols % NY
    xlo = rows // 2
    core = rows % 2
    sign = 1 - 2 * core

    def at(xh_, z_, y_):
        return (xh_ * NZ + z_) * NY + y_

    x_peer = (at(1 - xh, z, y), rows)
    z_peer = {d: (at(xh, (z + d * sign + NZ) % NZ, y), rows) for d in (1, -1)}
    y_peer = {d: (at(xh, z, (y + d * sign + NY) % NY), rows) for d in (1, -1)}
    core_peer = (cols, xlo * 2 + 1 - core)
    chip_peer = (cols, (1 - xlo) * 2 + core)

    grad_copy = pltpu.make_async_copy(grad_hbm, grad, local_sem.at[0])
    prior_copy = pltpu.make_async_copy(prior_hbm, update, local_sem.at[1])
    grad_copy.start()
    prior_copy.start()

    barrier = pltpu.get_barrier_semaphore()
    peers = [x_peer, z_peer[1], z_peer[-1], y_peer[1], y_peer[-1], core_peer, chip_peer]
    for peer in peers:
        pl.semaphore_signal(barrier, inc=1, device_id=peer, device_id_type=MESH)

    for c in range(GROUPS):
        for half in range(2):
            buf[c, xh, z, y, :, half * 128:(half + 1) * 128] = pieces[ids[c] * 2 + half]

    pl.semaphore_wait(barrier, len(peers))

    def remote(src, dst, c, number, peer):
        return pltpu.make_async_remote_copy(
            src_ref=src, dst_ref=dst, send_sem=send_sem.at[c, number], recv_sem=recv_sem.at[c, number],
            device_id=peer, device_id_type=MESH)

    def x_copy(c):
        ref = buf.at[c, xh, z, y]
        return remote(ref, ref, c, SEM_X, x_peer)

    for c in range(GROUPS):
        x_copy(c).start()

    def ring_copy(stream, c, d, i):
        k, h = i // 2, (i % 2 if d == 1 else 1 - i % 2)
        first, second = pl.ds(0, SPLIT[h]), pl.ds(SPLIT[h], PIECE - SPLIT[h])
        zk = (z - d * sign * k + NZ) % NZ
        yk = (y - d * sign * k + 2 * NY) % NY
        lane = 0 if d == 1 else 1
        if stream == "a1":
            ref, number, peer = buf.at[c, h, zk, y, first], SEM_A1 + 2 * i + lane, z_peer[d]
        elif stream == "b1":
            ref, number, peer = buf.at[c, h, z, yk, second], SEM_B1 + 2 * i + lane, y_peer[d]
        elif stream == "a2":
            ref, number, peer = buf.at[c, h, :, yk, first], SEM_A2 + 2 * i + lane, y_peer[d]
        else:
            ref, number, peer = buf.at[c, h, zk, :, second], SEM_B2 + 2 * i + lane, z_peer[d]
        return remote(ref, ref, c, number, peer)

    def run_tick(stream, ticks, c, t):
        if t in ticks:
            i = ticks.index(t)
            for d in (1, -1):
                if i >= 2:
                    ring_copy(stream, c, d, i - 2).wait_recv()
                ring_copy(stream, c, d, i).start()

    def finish(stream, ticks, c):
        for i in range(len(ticks) - 2, len(ticks)):
            for d in (1, -1):
                ring_copy(stream, c, d, i).wait_recv()

    def drain(stream, ticks, c):
        for i in range(len(ticks)):
            for d in (1, -1):
                ring_copy(stream, c, d, i).wait_send()

    def rows_of(n):
        return n // 4, pl.ds((n % 4) * 2, 2)

    def rotate(c, begin, count):
        def body(n, _):
            xn, zn = rows_of(n)
            high, low = split_terms(buf[c, xn, zn].reshape(256, GROUP))
            part = grad[pl.ds(n * 256, 256), :]
            dims = (((0,), (0,)), ((), ()))
            total = lax.dot_general(high, part, dims, preferred_element_type=jnp.float32)
            total += lax.dot_general(low, part, dims, preferred_element_type=jnp.float32)
            total = total.reshape(2, 2, QUARTER, COLS)

            @pl.when(n == 0)
            def _():
                partial[c] = total

            @pl.when(n > 0)
            def _():
                partial[c] += total
            return 0
        lax.fori_loop(begin, begin + count, body, 0)

    def rotate_back(c, last):
        a_high, a_low = split_terms(adjusted[c].reshape(GROUP, COLS))

        def body(n, _):
            xn, zn = rows_of(n)
            high, low = split_terms(buf[c, xn, zn].reshape(256, GROUP))
            here = pl.ds(n * 256, 256)
            total = jnp.dot(high, a_low, preferred_element_type=jnp.float32)
            total += jnp.dot(low, a_high, preferred_element_type=jnp.float32)
            total += jnp.dot(high, a_high, preferred_element_type=jnp.float32)
            update[here, :] += total

            @pl.when(last)
            def _():
                pltpu.make_async_copy(update.at[here], update_hbm.at[here], out_sem.at[n]).start()
            return 0
        lax.fori_loop(0, ROWS // 256, body, 0)

    def rs1_copy(c):
        return remote(partial.at[c, :, 1 - core], rs1.at[c], c, SEM_RS1, core_peer)

    def rs2_copy(c):
        return remote(xsend.at[c], rs2.at[c], c, SEM_RS2, chip_peer)

    def ax_copy(c):
        ref = adjusted.at[c, xlo, core]
        return remote(ref, ref, c, SEM_AX, chip_peer)

    def ac_copy(c):
        ref = adjusted.at[c, xlo, core]
        return remote(ref, ref, c, SEM_AC, core_peer)

    def af_copy(c):
        ref = adjusted.at[c, 1 - xlo, core]
        return remote(ref, ref, c, SEM_AF, core_peer)

    def moments(c):
        rotated = partial[c, xlo, core] + rs1[c, xlo] + rs2[c]
        one = beta_one * first_in[c] + (1.0 - beta_one) * rotated
        two = beta_two * second_in[c] + (1.0 - beta_two) * rotated * rotated
        first_out[c] = one
        second_out[c] = two
        adjusted[c, xlo, core] = one / correct_one / (jnp.sqrt(two / correct_two) + epsilon)

    def macro(m, _):
        do_p1 = m < GROUPS
        do_p2 = (m >= 1) & (m < GROUPS + 1)
        do_p2_left = (m >= 2) & (m < GROUPS + 2)
        do_mid = (m >= 2) & (m < GROUPS + 2)
        do_back = m >= 3
        s1, s2, s3, s4 = m, m - 1, m - 2, m - 3

        @pl.when(do_p1)
        def _():
            x_copy(s1).wait_recv()

        for t in range(TICKS):
            if t < TICKS - 1:
                @pl.when(do_p2)
                def _(t=t):
                    run_tick("b2", Z_TICKS, s2, t)
                    run_tick("a2", Y_BIG_TICKS, s2, t)

                @pl.when(do_p1)
                def _(t=t):
                    run_tick("a1", Z_TICKS, s1, t)
                    run_tick("b1", Y_SMALL_TICKS, s1, t)

            if t == 0:
                @pl.when(m == 2)
                def _():
                    grad_copy.wait()

                @pl.when(m == 3)
                def _():
                    prior_copy.wait()

                @pl.when(do_back)
                def _():
                    ac_copy(s4).wait_recv()
                    af_copy(s4).wait_recv()
                    rotate_back(s4, m == GROUPS + 2)
            if t == 1:
                @pl.when(do_p2_left)
                def _():
                    finish("a2", Y_BIG_TICKS, s3)
                    finish("b2", Z_TICKS, s3)
                    rotate(s3, 0, 4)
            if t == 2:
                @pl.when(do_mid)
                def _():
                    rotate(s3, 4, 4)
                    rs1_copy(s3).start()
            if t == 3:
                @pl.when(do_mid)
                def _():
                    rs1_copy(s3).wait_recv()
                    xsend[s3] = partial[s3, 1 - xlo, core] + rs1[s3, 1 - xlo]
                    rs2_copy(s3).start()
            if t == 5:
                @pl.when(do_mid)
                def _():
                    rs2_copy(s3).wait_recv()
                    moments(s3)
                    ax_copy(s3).start()
                    ac_copy(s3).start()
            if t == 7:
                @pl.when(do_p1)
                def _():
                    finish("a1", Z_TICKS, s1)
                    finish("b1", Y_SMALL_TICKS, s1)

                @pl.when(do_mid)
                def _():
                    ax_copy(s3).wait_recv()
                    af_copy(s3).start()
        return 0

    lax.fori_loop(0, GROUPS + 3, macro, 0)

    def last(c, _):
        x_copy(c).wait_send()
        drain("a1", Z_TICKS, c)
        drain("b1", Y_SMALL_TICKS, c)
        drain("a2", Y_BIG_TICKS, c)
        drain("b2", Z_TICKS, c)
        for copy in (rs1_copy, rs2_copy, ax_copy, ac_copy, af_copy):
            copy(c).wait_send()
        return 0

    lax.fori_loop(0, GROUPS, last, 0)

    def written(n, _):
        here = pl.ds(n * 256, 256)
        pltpu.make_async_copy(update.at[here], update_hbm.at[here], out_sem.at[n]).wait()
        return 0

    lax.fori_loop(0, ROWS // 256, written, 0)


def step(gradient, eigenbasis, first_moment, second_moment, prior_update, group_ids):
    pieces = lax.all_to_all(
        eigenbasis.reshape(NX * NZ * NY, PIECE, 128), "cols", 0, 0, tiled=True)
    vmem = pl.BlockSpec(memory_space=pltpu.VMEM)
    hbm = pl.BlockSpec(memory_space=pl.ANY)
    block = (GROUPS, QUARTER, COLS)
    return pl.pallas_call(
        kernel,
        out_shape=(
            jax.ShapeDtypeStruct(block, jnp.float32),
            jax.ShapeDtypeStruct(block, jnp.float32),
            jax.ShapeDtypeStruct((ROWS, COLS), jnp.float32),
        ),
        in_specs=[pl.BlockSpec(memory_space=pltpu.SMEM), vmem, vmem, vmem, hbm, hbm],
        out_specs=(vmem, vmem, hbm),
        scratch_shapes=[
            pltpu.VMEM((GROUPS, NX, NZ, NY, PIECE, GROUP), jnp.float32),
            pltpu.VMEM((ROWS, COLS), jnp.bfloat16),
            pltpu.VMEM((ROWS, COLS), jnp.float32),
            pltpu.VMEM((GROUPS, 2, 2, QUARTER, COLS), jnp.float32),
            pltpu.VMEM((GROUPS, 2, QUARTER, COLS), jnp.float32),
            pltpu.VMEM(block, jnp.float32),
            pltpu.VMEM(block, jnp.float32),
            pltpu.VMEM((GROUPS, 2, 2, QUARTER, COLS), jnp.float32),
            pltpu.SemaphoreType.DMA((GROUPS, SEMS)),
            pltpu.SemaphoreType.DMA((GROUPS, SEMS)),
            pltpu.SemaphoreType.DMA((2,)),
            pltpu.SemaphoreType.DMA((ROWS // 256,)),
        ],
        compiler_params=pltpu.CompilerParams(
            collective_id=0, has_side_effects=True, vmem_limit_bytes=50 * 1024 * 1024),
        cost_estimate=pl.CostEstimate(flops=9_400_000_000, bytes_accessed=14_000_000, transcendentals=0),
    )(group_ids, pieces, first_moment, second_moment, gradient, prior_update)


def solution(mesh):
    split = P("rows", "cols")
    moment = P(None, "rows", "cols")
    return jax.shard_map(
        step, mesh=mesh,
        in_specs=(split, split, moment, moment, split, P(None)),
        out_specs=(moment, moment, split),
        check_vma=False,
    )
```

time: 676 us -> 166 us (0.25)
  waiting for transfers between devices: 569 us -> 19.2 us
  Pallas kernels: 0 us -> 115 us
  matrix products: 39.3 us -> 0 us
  blocking collectives: 29.5 us -> 0 us
  between operations: 16.9 us -> 0.65 us
  local copies, waits for them, and re-layouts: 2.61 us -> 15.9 us
    dynamic_slice x4 -> x0, waiting for transfers between devices: 450 us -> none  [reference(): group_basis = lax.dynamic_slice_in_dim(eigenbasis, begin, GROUP, 1)]
    pallas_call x0 -> x1, Pallas kernels: none -> 115 us  [step(): pl.pallas_call(kernel, out_shape=(jax.ShapeDtypeStruct(block, jnp.float32...]
    unnamed x12 -> x0, waiting for transfers between devices: 93.7 us -> none
    dot_general x8 -> x0, matrix products: 39.3 us -> none  [the longest x4 23.3 us: reference(): jnp.dot(group_basis.T, grad_float, precision=lax.Precision.HIGHEST, prefe...]
    div x4 -> x0, blocking collectives: 29.5 us -> none  [reference(): moment_one / correct_one / (jnp.sqrt(moment_two / correct_two) + epsilon)]
    another operation x1 -> x0, waiting for transfers between devices: 24.9 us -> none
    all_to_all x0 -> x1, waiting for transfers between devices: none -> 19.2 us  [step(): lax.all_to_all(eigenbasis.reshape(NX * NZ * NY, PIECE, 128), 'cols', 0, 0...]
    another operation x1 -> x0, starting transfers between devices: 15.3 us -> none
  transfers between devices with their start and end apart: 9 -> 1, of which waited for: 9 -> 1; matrix products, arithmetic and copies ran while one was open for 4% -> 5% of each run, Pallas kernels for 0% -> 0%
where the time goes in v1:
time: 166 us
  Pallas kernels  115 us (69%)
  waiting for transfers between devices  19.2 us (12%)
  local copies, waits for them, and re-layouts  15.9 us (10%)
  starting transfers between devices  15.1 us (9%)
    pallas_call x1, Pallas kernels, step(): pl.pallas_call(kernel, out_shape=(jax.ShapeDtypeStruct(block, jnp.float32...  115 us
    all_to_all x1, waiting for transfers between devices, step(): lax.all_to_all(eigenbasis.reshape(NX * NZ * NY, PIECE, 128), 'cols', 0, 0...  19.2 us
    all_to_all x1, starting transfers between devices, step(): lax.all_to_all(eigenbasis.reshape(NX * NZ * NY, PIECE, 128), 'cols', 0, 0...  15.1 us
    unnamed x10, local copies, waits for them, and re-layouts  10.6 us
    pallas_call x1, local copies, waits for them, and re-layouts, step(): pl.pallas_call(kernel, out_shape=(jax.ShapeDtypeStruct(block, jnp.float32...  5.27 us
  transfers between devices with their start and end apart: 1, of which 1 were waited for; matrix products, arithmetic and copies ran while one was open for 5% of the time, Pallas kernels for 0%

profile of v1, /device:TPU:1, one launch (start us, length us, event | category | flops | bytes accessed | tf_op | source)
XLA Modules:
  0.0 165.9 jit_solution(17868707117821080815)
XLA Ops:
  0.6 15.1 %all-to-all-start = ((f32[64,32,128]{2,1,0:T(8,128)}), f32[64,32,128]{2,1,0:T(8,128)S(1)}, u32[]{:S(2)}, u32[]{:S(2)}) async-start(f32[64,32,128]{2,1,0:T(8,128)} %bitcast.1), calls=%async_computation | async-start | bytes 2097152 | tf_op jit(solution)/shard_map/all_to_all | solution.py:301
  15.8 3.8 %copy.9.grad_hbm = bf16[2048,448]{1,0:T(8,128)(2,1)} copy(bf16[2048,448]{0,1:T(8,128)(2,1)} %param.6) | data formatting | bytes 3670016 | tf_op args[0]
  19.6 0.0 copy-start
  19.6 0.0 copy-start.1
  19.6 0.0 copy-start.2
  19.6 5.2 %copy.10.prior_hbm = f32[2048,448]{1,0:T(8,128)} copy(f32[2048,448]{0,1:T(8,128)} %param.10) | data formatting | bytes 7340032 | tf_op args[4]
  24.8 19.2 %all-to-all-done.pieces = f32[64,32,128]{2,1,0:T(8,128)S(1)} async-done(((f32[64,32,128]{2,1,0:T(8,128)}), f32[64,32,128]{2,1,0:T(8,128)S(1)}, u32[]{:S(2)}, u32[]{:S(2)}) %all-to-all-start) | async-done | bytes 1048608 | tf_op jit(solution)/shard_map/all_to_all | solution.py:301
  44.0 0.0 copy-done
  44.0 0.0 copy-done.1
  44.0 0.0 copy-done.2
  44.0 115.0 %shard_map.85 = (f32[4,64,448]{2,1,0:T(8,128)S(1)}, f32[4,64,448]{2,1,0:T(8,128)S(1)}, f32[2048,448]{1,0:T(8,128)}) custom-call(s32[4]{0:T(128)S(1)} %copy-done.2, f32[64,32,128]{2,1,0:T(8,128)S(1)} %all-to-all-done.pieces, f32[4,64,448]{2,1,0:T(8,128)S(1)} %copy-done, f32[4,64,448]{2,1,0:T(8,128)S(1)} %copy-done.1, bf16[2048,448]{1,0:T(8,128)(2,1)} %copy.9.grad_hbm, ...), custom_call_target="tpu_custom_call" | custom-call | flops 9400000512 | bytes 14000000 | tf_op jit(solution)/shard_map/pallas_call | solution.py:306
  159.1 5.3 %copy.11 = f32[2048,448]{0,1:T(8,128)} copy(f32[2048,448]{1,0:T(8,128)} %get-tuple-element.5) | data formatting | bytes 7340032 | tf_op jit(solution)/shard_map/pallas_call | solution.py:306
  164.3 0.8 copy.14
  165.1 0.8 copy.15
Async XLA Ops:
  0.6 43.4 %all-to-all-start = ((f32[64,32,128]{2,1,0:T(8,128)}), f32[64,32,128]{2,1,0:T(8,128)S(1)}, u32[]{:S(2)}, u32[]{:S(2)}) async-start(f32[64,32,128]{2,1,0:T(8,128)} %bitcast.1), calls=%async_computation | async-start | bytes 2097152 | tf_op jit(solution)/shard_map/all_to_all | solution.py:301
  19.6 24.4 %copy-start = (f32[4,64,448]{2,1,0:T(8,128)S(1)}, f32[4,64,448]{2,1,0:T(8,128)}, u32[]{:S(2)}) copy-start(f32[4,64,448]{2,1,0:T(8,128)} %first_in.1) | copy-start | bytes 1376260
  19.6 24.4 %copy-start.1 = (f32[4,64,448]{2,1,0:T(8,128)S(1)}, f32[4,64,448]{2,1,0:T(8,128)}, u32[]{:S(2)}) copy-start(f32[4,64,448]{2,1,0:T(8,128)} %second_in.1) | copy-start | bytes 1376260
  19.6 24.4 %copy-start.2 = (s32[4]{0:T(128)S(1)}, s32[4]{0:T(128)}, u32[]{:S(2)}) copy-start(s32[4]{0:T(128)} %ids.1) | copy-start | bytes 52

commit v2 on v0

v2 whole, which is shorter than its diff:
```python
import functools

import jax
import jax.numpy as jnp
from jax import lax
from jax.experimental import pallas as pl
from jax.experimental.pallas import tpu as pltpu
from jax.sharding import PartitionSpec as P

MESH = pl.DeviceIdType.MESH

GROUPS = 4
NX, NZ, NY = 2, 8, 4
SPREAD = NX * NZ * NY
PIECE = 32
GROUP = 256
QUARTER = 64
COLS = 448
ROWS = 2048

beta_one = 0.9
beta_two = 0.95
correct_one = 1.0 - 0.9**10
correct_two = 1.0 - 0.95**10
epsilon = 1e-08

FIRST, SECOND = pl.ds(0, 16), pl.ds(16, 16)

SEM_X = 0
SEM_A1 = 1
SEM_B1 = SEM_A1 + 16
SEM_A2 = SEM_B1 + 8
SEM_B2 = SEM_A2 + 4
SEM_RS1 = SEM_B2 + 8
SEM_RS2 = SEM_RS1 + 1
SEM_AX = SEM_RS2 + 1
SEM_AC = SEM_AX + 1
SEM_AF = SEM_AC + 1
SEMS = SEM_AF + 1


def split_terms(value):
    high = value.astype(jnp.bfloat16)
    low = (value - high.astype(jnp.float32)).astype(jnp.bfloat16)
    return high, low


def kernel(ids, basis_hbm, first_in, second_in, grad_hbm, prior_hbm,
           first_out, second_out, update_hbm,
           pieces, buf, grad, update, rotated, partial, rs1, xsend, rs2, adjusted,
           send_sem, recv_sem, local_sem, out_sem, deal_send, deal_recv):
    cols = lax.axis_index("cols")
    rows = lax.axis_index("rows")
    xh = cols // (NZ * NY)
    z = (cols // NY) % NZ
    y = cols % NY
    xlo = rows // 2
    core = rows % 2
    sign = 1 - 2 * core

    def at(xh_, z_, y_):
        return (xh_ * NZ + z_) * NY + y_

    x_peer = (at(1 - xh, z, y), rows)
    z_peer = {d: (at(xh, (z + d * sign + NZ) % NZ, y), rows) for d in (1, -1)}
    y_peer = {d: (at(xh, z, (y + d * sign + NY) % NY), rows) for d in (1, -1)}
    core_peer = (cols, xlo * 2 + 1 - core)
    chip_peer = (cols, (1 - xlo) * 2 + core)

    grad_copy = pltpu.make_async_copy(grad_hbm, grad, local_sem.at[0])
    prior_copy = pltpu.make_async_copy(prior_hbm, update, local_sem.at[1])

    barrier = pltpu.get_barrier_semaphore()
    for peer in (core_peer, chip_peer):
        pl.semaphore_signal(barrier, inc=1, device_id=peer, device_id_type=MESH)

    def greet(n, _):
        pl.semaphore_signal(barrier, inc=1, device_id=((cols + n) % SPREAD, rows), device_id_type=MESH)
        return 0

    lax.fori_loop(1, SPREAD, greet, 0)
    pl.semaphore_wait(barrier, SPREAD + 1)

    def deal(n, _):
        to = (cols + n) % SPREAD
        pltpu.make_async_remote_copy(
            src_ref=basis_hbm.at[to], dst_ref=pieces.at[cols], send_sem=deal_send, recv_sem=deal_recv,
            device_id=(to, rows), device_id_type=MESH).start()
        return 0

    lax.fori_loop(1, SPREAD, deal, 0)
    own_piece = pltpu.make_async_copy(basis_hbm.at[cols], pieces.at[cols], local_sem.at[2])
    own_piece.start()
    grad_copy.start()
    prior_copy.start()
    own_piece.wait()
    others = pl.ds(0, SPREAD - 1)
    dealt = pltpu.make_async_remote_copy(
        src_ref=basis_hbm.at[others], dst_ref=pieces.at[others], send_sem=deal_send, recv_sem=deal_recv,
        device_id=((cols + 1) % SPREAD, rows), device_id_type=MESH)
    dealt.wait_recv()

    for c in range(GROUPS):
        for half in range(2):
            buf[c, xh, z, y, :, half * 128:(half + 1) * 128] = pieces[ids[c] * 2 + half]

    def remote(src, dst, c, number, peer):
        return pltpu.make_async_remote_copy(
            src_ref=src, dst_ref=dst, send_sem=send_sem.at[c, number], recv_sem=recv_sem.at[c, number],
            device_id=peer, device_id_type=MESH)

    def x_copy():
        ref = buf.at[:, xh, z, y]
        return remote(ref, ref, 0, SEM_X, x_peer)

    own, other = xh, 1 - xh

    def zk(d, k):
        return (z - d * sign * k + NZ) % NZ

    def yk(d, k):
        return (y - d * sign * k + 2 * NY) % NY

    def spread_z(half, d, k):
        which, lane = (0, own) if half == 0 else (1, other)
        ref = buf.at[:, lane, zk(d, k), y, FIRST]
        return remote(ref, ref, 0, SEM_A1 + which * 8 + (0 if d == 1 else 4) + k, z_peer[d])

    def spread_y(half, d, k):
        which, lane = (0, own) if half == 0 else (1, other)
        ref = buf.at[:, lane, z, yk(d, k), SECOND]
        return remote(ref, ref, 0, SEM_B1 + which * 4 + (0 if d == 1 else 2) + k, y_peer[d])

    z_steps = [(half, d, k) for k in range(4) for half in range(2) for d in (1, -1)
               if k < 3 or (half == 0) == (d == 1)]
    y_steps = [(half, d, k) for k in range(2) for half in range(2) for d in (1, -1)
               if k < 1 or (half == 0) == (d == 1)]

    def lanes(d, whole):
        return slice(None) if whole else (0 if d == 1 else 1)

    def gather_z(c, d, k):
        ref = buf.at[c, lanes(d, k < 3), zk(d, k), :, SECOND]
        return remote(ref, ref, c, SEM_B2 + (0 if d == 1 else 4) + k, z_peer[d])

    def gather_y(c, d, k):
        ref = buf.at[c, lanes(d, k < 1), :, yk(d, k), FIRST]
        return remote(ref, ref, c, SEM_A2 + (0 if d == 1 else 2) + k, y_peer[d])

    def both(make, c, k, action):
        for d in (1, -1):
            getattr(make(c, d, k), action)()

    def rows_of(n):
        return n // 4, pl.ds((n % 4) * 2, 2)

    def rotate(c, half):
        high, low = split_terms(buf[c, half].reshape(ROWS // 2, GROUP))
        part = grad[:, half * (ROWS // 2):(half + 1) * (ROWS // 2)]
        total = jnp.dot(part, high, preferred_element_type=jnp.float32)
        total += jnp.dot(part, low, preferred_element_type=jnp.float32)
        if half == 0:
            rotated[...] = total
        else:
            partial[c] = (rotated[...] + total).T.reshape(2, 2, QUARTER, COLS)

    def rotate_back(c, last):
        a_high, a_low = split_terms(adjusted[c].reshape(GROUP, COLS).T)
        dims = (((1,), (1,)), ((), ()))

        def body(n, _):
            xn, zn = rows_of(n)
            high, low = split_terms(buf[c, xn, zn].reshape(256, GROUP))
            here = pl.ds(pl.multiple_of(n * 256, 256), 256)
            total = lax.dot_general(a_low, high, dims, preferred_element_type=jnp.float32)
            total += lax.dot_general(a_high, low, dims, preferred_element_type=jnp.float32)
            total += lax.dot_general(a_high, high, dims, preferred_element_type=jnp.float32)
            update[:, here] += total

            if last:
                pltpu.make_async_copy(update.at[:, here], update_hbm.at[:, here], out_sem.at[n]).start()
            return 0
        lax.fori_loop(0, ROWS // 256, body, 0)

    def rs1_copy(c):
        return remote(partial.at[c, :, 1 - core], rs1.at[c], c, SEM_RS1, core_peer)

    def rs2_copy(c):
        return remote(xsend.at[c], rs2.at[c], c, SEM_RS2, chip_peer)

    def ax_copy(c):
        ref = adjusted.at[c, xlo, core]
        return remote(ref, ref, c, SEM_AX, chip_peer)

    def ac_copy(c):
        ref = adjusted.at[c, xlo, core]
        return remote(ref, ref, c, SEM_AC, core_peer)

    def af_copy(c):
        ref = adjusted.at[c, 1 - xlo, core]
        return remote(ref, ref, c, SEM_AF, core_peer)

    def moments(c):
        mine = partial[c, xlo, core] + rs1[c, xlo] + rs2[c]
        one = beta_one * first_in[c] + (1.0 - beta_one) * mine
        two = beta_two * second_in[c] + (1.0 - beta_two) * mine * mine
        first_out[c] = one
        second_out[c] = two
        adjusted[c, xlo, core] = one / correct_one / (jnp.sqrt(two / correct_two) + epsilon)

    def z_step(c, k):
        if k > 0:
            both(gather_z, c, k - 1, "wait_recv")
        both(gather_z, c, k, "start")

    def y_step(c, k):
        if k > 0:
            both(gather_y, c, k - 1, "wait_recv")
        both(gather_y, c, k, "start")

    def arrive(c):
        both(gather_z, c, 3, "wait_recv")
        both(gather_y, c, 1, "wait_recv")
        rotate(c, 0)
        rotate(c, 1)
        rs1_copy(c).start()

    def cross(c):
        rs1_copy(c).wait_recv()
        xsend[c] = partial[c, 1 - xlo, core] + rs1[c, 1 - xlo]
        rs2_copy(c).start()

    def adjust(c):
        rs2_copy(c).wait_recv()
        moments(c)
        ax_copy(c).start()
        ac_copy(c).start()

    def forward(c):
        ax_copy(c).wait_recv()
        af_copy(c).start()

    def back(c):
        ac_copy(c).wait_recv()
        af_copy(c).wait_recv()
        rotate_back(c, c == GROUPS - 1)

    def spread_step(make, steps, k):
        for half in range(2):
            for d in (1, -1):
                if k > 0 and (half, d, k - 1) in steps:
                    make(half, d, k - 1).wait_recv()
                if (half, d, k) in steps:
                    make(half, d, k).start()

    x_copy().start()
    for half in range(2):
        if half == 1:
            x_copy().wait_recv()
        for d in (1, -1):
            spread_z(half, d, 0).start()
            spread_y(half, d, 0).start()
    spread_step(spread_y, y_steps, 1)
    spread_step(spread_z, z_steps, 1)
    spread_step(spread_y, y_steps, 2)
    z_step(0, 0)
    spread_step(spread_z, z_steps, 2)
    z_step(1, 0)
    spread_step(spread_z, z_steps, 3)
    z_step(0, 1)
    spread_step(spread_z, z_steps, 4)

    y_step(0, 0)
    z_step(1, 1)
    z_step(0, 2)
    y_step(1, 0)
    z_step(2, 0)
    y_step(0, 1)
    z_step(0, 3)
    z_step(1, 2)
    y_step(2, 0)
    z_step(2, 1)
    y_step(1, 1)
    z_step(1, 3)
    z_step(3, 0)
    grad_copy.wait()
    prior_copy.wait()
    arrive(0)
    z_step(2, 2)
    y_step(3, 0)
    cross(0)
    z_step(3, 1)
    y_step(2, 1)
    arrive(1)
    adjust(0)
    z_step(2, 3)
    cross(1)
    z_step(3, 2)
    y_step(3, 1)
    forward(0)
    arrive(2)
    adjust(1)
    back(0)
    z_step(3, 3)
    cross(2)
    forward(1)
    adjust(2)
    arrive(3)
    back(1)
    cross(3)
    forward(2)
    back(2)
    adjust(3)
    forward(3)
    back(3)

    dealt.wait_send()
    x_copy().wait_send()
    for step_ in z_steps:
        spread_z(*step_).wait_send()
    for step_ in y_steps:
        spread_y(*step_).wait_send()

    def last(c, _):
        for k in range(4):
            both(gather_z, c, k, "wait_send")
        for k in range(2):
            both(gather_y, c, k, "wait_send")
        for copy in (rs1_copy, rs2_copy, ax_copy, ac_copy, af_copy):
            copy(c).wait_send()
        return 0

    lax.fori_loop(0, GROUPS, last, 0)

    def written(n, _):
        here = pl.ds(pl.multiple_of(n * 256, 256), 256)
        pltpu.make_async_copy(update.at[:, here], update_hbm.at[:, here], out_sem.at[n]).wait()
        return 0

    lax.fori_loop(0, ROWS // 256, written, 0)


def step(gradient, eigenbasis, first_moment, second_moment, prior_update, group_ids):
    pieces = eigenbasis.reshape(SPREAD, PIECE, 128)
    vmem = pl.BlockSpec(memory_space=pltpu.VMEM)
    hbm = pl.BlockSpec(memory_space=pl.ANY)
    block = (GROUPS, QUARTER, COLS)
    first_out, second_out, update = pl.pallas_call(
        kernel,
        out_shape=(
            jax.ShapeDtypeStruct(block, jnp.float32),
            jax.ShapeDtypeStruct(block, jnp.float32),
            jax.ShapeDtypeStruct((COLS, ROWS), jnp.float32),
        ),
        in_specs=[pl.BlockSpec(memory_space=pltpu.SMEM), hbm, vmem, vmem, hbm, hbm],
        out_specs=(vmem, vmem, hbm),
        scratch_shapes=[
            pltpu.VMEM((SPREAD, PIECE, 128), jnp.float32),
            pltpu.VMEM((GROUPS, NX, NZ, NY, PIECE, GROUP), jnp.float32),
            pltpu.VMEM((COLS, ROWS), jnp.bfloat16),
            pltpu.VMEM((COLS, ROWS), jnp.float32),
            pltpu.VMEM((COLS, GROUP), jnp.float32),
            pltpu.VMEM((GROUPS, 2, 2, QUARTER, COLS), jnp.float32),
            pltpu.VMEM((GROUPS, 2, QUARTER, COLS), jnp.float32),
            pltpu.VMEM(block, jnp.float32),
            pltpu.VMEM(block, jnp.float32),
            pltpu.VMEM((GROUPS, 2, 2, QUARTER, COLS), jnp.float32),
            pltpu.SemaphoreType.DMA((GROUPS, SEMS)),
            pltpu.SemaphoreType.DMA((GROUPS, SEMS)),
            pltpu.SemaphoreType.DMA((3,)),
            pltpu.SemaphoreType.DMA((ROWS // 256,)),
            pltpu.SemaphoreType.DMA,
            pltpu.SemaphoreType.DMA,
        ],
        compiler_params=pltpu.CompilerParams(
            collective_id=0, has_side_effects=True, vmem_limit_bytes=50 * 1024 * 1024),
        cost_estimate=pl.CostEstimate(flops=9_400_000_000, bytes_accessed=14_000_000, transcendentals=0),
    )(group_ids, pieces, first_moment, second_moment, gradient.T, prior_update.T)
    return first_out, second_out, update.T


def solution(mesh):
    split = P("rows", "cols")
    moment = P(None, "rows", "cols")
    return jax.shard_map(
        step, mesh=mesh,
        in_specs=(split, split, moment, moment, split, P(None)),
        out_specs=(moment, moment, split),
        check_vma=False,
    )
```

time: 676 us -> 139 us (0.21)
  waiting for transfers between devices: 569 us -> 0 us
  Pallas kernels: 0 us -> 128 us
  matrix products: 39.3 us -> 0 us
  blocking collectives: 29.5 us -> 0 us
  between operations: 16.9 us -> 0.65 us
  starting transfers between devices: 15.8 us -> 0 us
  local copies, waits for them, and re-layouts: 2.61 us -> 9.84 us
    dynamic_slice x4 -> x0, waiting for transfers between devices: 450 us -> none  [reference(): group_basis = lax.dynamic_slice_in_dim(eigenbasis, begin, GROUP, 1)]
    pallas_call x0 -> x1, Pallas kernels: none -> 128 us  [step(): pl.pallas_call(kernel, out_shape=(jax.ShapeDtypeStruct(block, jnp.float32...]
    unnamed x12 -> x0, waiting for transfers between devices: 93.7 us -> none
    dot_general x8 -> x0, matrix products: 39.3 us -> none  [the longest x4 23.3 us: reference(): jnp.dot(group_basis.T, grad_float, precision=lax.Precision.HIGHEST, prefe...]
    div x4 -> x0, blocking collectives: 29.5 us -> none  [reference(): moment_one / correct_one / (jnp.sqrt(moment_two / correct_two) + epsilon)]
    another operation x1 -> x0, waiting for transfers between devices: 24.9 us -> none
    another operation x1 -> x0, starting transfers between devices: 15.3 us -> none
    unnamed x21 -> x11, local copies, waits for them, and re-layouts: 0.66 us -> 9.84 us
  transfers between devices with their start and end apart: 9 -> 0, of which waited for: 9 -> 0; matrix products, arithmetic and copies ran while one was open for 4% -> 0% of each run, Pallas kernels for 0% -> 0%
where the time goes in v2:
time: 139 us
  Pallas kernels  128 us (92%)
  local copies, waits for them, and re-layouts  9.84 us (7%)
    pallas_call x1, Pallas kernels, step(): pl.pallas_call(kernel, out_shape=(jax.ShapeDtypeStruct(block, jnp.float32...  128 us
    unnamed x11, local copies, waits for them, and re-layouts  9.84 us

profile of v2, /device:TPU:1, one launch (start us, length us, event | category | flops | bytes accessed | tf_op | source)
XLA Modules:
  0.0 138.5 jit_solution(298624646712279375)
XLA Ops:
  0.6 0.0 copy-start
  0.6 1.2 copy-done
  1.9 0.0 copy-start.1
  1.9 1.0 copy-done.1
  2.9 0.0 copy-start.2
  2.9 1.0 copy-done.2
  3.9 0.0 copy-start.3
  3.9 0.7 copy-done.3
  4.6 128.0 %shard_map.85 = (f32[4,64,448]{2,1,0:T(8,128)S(1)}, f32[4,64,448]{2,1,0:T(8,128)S(1)}, f32[448,2048]{1,0:T(8,128)}) custom-call(s32[4]{0:T(128)S(1)} %copy-done.3, f32[64,32,128]{2,1,0:T(8,128)S(1)} %bitcast.4, f32[4,64,448]{2,1,0:T(8,128)S(1)} %copy-done.1, f32[4,64,448]{2,1,0:T(8,128)S(1)} %copy-done.2, bf16[448,2048]{1,0:T(8,128)(2,1)} %bitcast.7, ...), custom_call_target="tpu_custom_call" | custom-call | flops 9400000512 | bytes 14000000 | tf_op jit(solution)/shard_map/pallas_call | solution.py:348
  132.6 0.8 copy.12
  133.4 0.8 copy.13
  134.2 4.3 %copy.14 = f32[2048,448]{0,1:T(8,128)} copy(f32[2048,448]{0,1:T(8,128)} %bitcast.5) | data formatting | bytes 7340032
Async XLA Ops:
  0.6 1.2 copy-start
  1.9 1.0 copy-start.1
  2.9 1.0 copy-start.2
  3.9 0.7 copy-start.3

commit v3 on v2

v3 whole, which is shorter than its diff:
```python
import functools

import jax
import jax.numpy as jnp
from jax import lax
from jax.experimental import pallas as pl
from jax.experimental.pallas import tpu as pltpu
from jax.sharding import PartitionSpec as P

MESH = pl.DeviceIdType.MESH

GROUPS = 4
NX, NZ, NY = 2, 8, 4
SPREAD = NX * NZ * NY
PIECE = 32
GROUP = 256
QUARTER = 64
COLS = 448
ROWS = 2048

beta_one = 0.9
beta_two = 0.95
correct_one = 1.0 - 0.9**10
correct_two = 1.0 - 0.95**10
epsilon = 1e-08

FIRST, SECOND = pl.ds(0, 16), pl.ds(16, 16)

SEM_A2 = 0
SEM_B2 = SEM_A2 + 4
SEM_RS1 = SEM_B2 + 8
SEM_RS2 = SEM_RS1 + 1
SEM_AX = SEM_RS2 + 2
SEM_AC = SEM_AX + 2
SEM_AF = SEM_AC + 2
SEMS = SEM_AF + 2


def split_terms(value):
    high = value.astype(jnp.bfloat16)
    low = (value - high.astype(jnp.float32)).astype(jnp.bfloat16)
    return high, low


def back_product(a_high, a_low, high, low):
    dims = (((1,), (1,)), ((), ()))
    total = lax.dot_general(a_low, high, dims, preferred_element_type=jnp.float32)
    total += lax.dot_general(a_high, low, dims, preferred_element_type=jnp.float32)
    return total + lax.dot_general(a_high, high, dims, preferred_element_type=jnp.float32)


def kernel(ids, basis_hbm, first_hbm, second_hbm, grad_hbm, prior_hbm,
           first_out, second_out, update, terms_out, adjusted_out,
           pieces, buf, grad, rotated, partial, rs1, xsend, rs2, adjusted,
           send_sem, recv_sem, local_sem, deal_send, deal_recv,
           spread_send, spread_recv, first_in, second_in, met):
    cols = lax.axis_index("cols")
    rows = lax.axis_index("rows")
    xh = cols // (NZ * NY)
    z = (cols // NY) % NZ
    y = cols % NY
    xlo = rows // 2
    core = rows % 2
    sign = 1 - 2 * core

    def at(xh_, z_, y_):
        return (xh_ * NZ + z_) * NY + y_

    x_peer = (at(1 - xh, z, y), rows)
    z_peer = {d: (at(xh, (z + d * sign + NZ) % NZ, y), rows) for d in (1, -1)}
    y_peer = {d: (at(xh, z, (y + d * sign + NY) % NY), rows) for d in (1, -1)}
    core_peer = (cols, xlo * 2 + 1 - core)
    chip_peer = (cols, (1 - xlo) * 2 + core)

    grad_copy = pltpu.make_async_copy(grad_hbm, grad, local_sem.at[0])
    prior_copy = pltpu.make_async_copy(prior_hbm, update, local_sem.at[1])
    first_copy = pltpu.make_async_copy(first_hbm, first_in, local_sem.at[3])
    second_copy = pltpu.make_async_copy(second_hbm, second_in, local_sem.at[4])

    def place(j, k, l):
        return (((xh + j) % NX) * NZ + (z + k) % NZ) * NY + (y + l) % NY

    def deal(j, k, l):
        to = place(j, k, l)
        pltpu.make_async_remote_copy(
            src_ref=basis_hbm.at[to], dst_ref=pieces.at[cols], send_sem=deal_send, recv_sem=deal_recv,
            device_id=(to, rows), device_id_type=MESH).start()

    line = [(0, k, 0) for k in range(1, NZ)] + [(0, 0, l) for l in range(1, NY)] + [(1, 0, 0)]
    barrier = pltpu.get_barrier_semaphore()
    for offsets in line:
        pl.semaphore_signal(barrier, inc=1, device_id=(place(*offsets), rows), device_id_type=MESH)
    for peer in (core_peer, chip_peer):
        pl.semaphore_signal(barrier, inc=1, device_id=peer, device_id_type=MESH)
    pl.semaphore_wait(barrier, len(line) + 2)
    for l in range(1, NY):
        pl.semaphore_signal(met.at[0], inc=1, device_id=(place(0, 0, l), rows), device_id_type=MESH)
    for offsets in line:
        deal(*offsets)
    pl.semaphore_wait(met.at[0], NY - 1)
    pl.semaphore_signal(met.at[1], inc=1, device_id=x_peer, device_id_type=MESH)
    for k in range(1, NZ):
        for l in range(1, NY):
            deal(0, k, l)
    pl.semaphore_wait(met.at[1], 1)
    for k in range(NZ):
        for l in range(NY):
            if (k, l) != (0, 0):
                deal(1, k, l)
    own_piece = pltpu.make_async_copy(basis_hbm.at[cols], pieces.at[cols], local_sem.at[2])
    own_piece.start()
    grad_copy.start()
    prior_copy.start()
    first_copy.start()
    second_copy.start()
    own_piece.wait()
    others = pl.ds(0, SPREAD - 1)
    dealt = pltpu.make_async_remote_copy(
        src_ref=basis_hbm.at[others], dst_ref=pieces.at[others], send_sem=deal_send, recv_sem=deal_recv,
        device_id=((cols + 1) % SPREAD, rows), device_id_type=MESH)
    dealt.wait_recv()

    for c in range(GROUPS):
        for half in range(2):
            buf[c, xh, z, y, :, half * 128:(half + 1) * 128] = pieces[ids[c] * 2 + half]

    def remote(src, dst, c, number, peer):
        return pltpu.make_async_remote_copy(
            src_ref=src, dst_ref=dst, send_sem=send_sem.at[c, number], recv_sem=recv_sem.at[c, number],
            device_id=peer, device_id_type=MESH)

    def zk(d, k):
        return (z - d * sign * k + NZ) % NZ

    def yk(d, k):
        return (y - d * sign * k + 2 * NY) % NY

    def spread(src, p, number, peer):
        return pltpu.make_async_remote_copy(
            src_ref=src, dst_ref=src, send_sem=spread_send.at[p, number], recv_sem=spread_recv.at[p, number],
            device_id=peer, device_id_type=MESH)

    def z_block(p, j):
        return buf.at[pl.ds(2 * p, 2), xh, zk(1, -j), y, FIRST]

    def z_near(p, j):
        return spread(z_block(p, 0), p, 2 + j if j < 0 else 1 + j, (at(xh, zk(1, -j), y), rows))

    def z_third(p, d):
        return spread(z_block(p, -2 * d), p, 4 if d == 1 else 5, (at(xh, zk(1, -d), y), rows))

    def z_fourth(p, d):
        src = buf.at[2 * p + (0 if d == 1 else 1), xh, zk(1, 2 * d), y, FIRST]
        return spread(src, p, 6 if d == 1 else 7, (at(xh, zk(1, -2 * d), y), rows))

    def z_across(p, j):
        return spread(z_block(p, j), p, 8 + j % NZ, x_peer)

    def y_near(p, j):
        return spread(buf.at[pl.ds(2 * p, 2), xh, z, y, SECOND], p, 15 + j, (at(xh, z, (y + j) % NY), rows))

    def y_across(p):
        return spread(buf.at[pl.ds(2 * p, 2), xh, z, :, SECOND], p, 19, x_peer)

    def spread_begin(p):
        for j in (1, 2, 3):
            y_near(p, j).start()
        for j in (1, -1, 2, -2):
            z_near(p, j).start()
        z_across(p, 0).start()

    def spread_y(p):
        for j in (1, 2, 3):
            y_near(p, j).wait_recv()
        y_across(p).start()

    def spread_z(p):
        for d in (1, -1):
            z_near(p, 2 * d).wait_recv()
            z_third(p, d).start()
            z_fourth(p, d).start()
            z_across(p, -2 * d).start()
        for d in (1, -1):
            z_near(p, d).wait_recv()
            z_across(p, -d).start()

    def spread_far(p):
        for d in (1, -1):
            z_third(p, d).wait_recv()
            z_across(p, -3 * d).start()
        for d in (1, -1):
            z_fourth(p, d).wait_recv()
        z_across(p, 4).start()

    def spread_z_ready(p):
        for j in (0, -2, 2, -1, 1, -3, 3, 4):
            z_across(p, j).wait_recv()

    def spread_drain(p):
        for d in (1, -1):
            for copy in (z_near(p, d), z_near(p, 2 * d), z_third(p, d), z_fourth(p, d)):
                copy.wait_send()
        for j in range(NZ):
            z_across(p, j - 3).wait_send()
        for j in (1, 2, 3):
            y_near(p, j).wait_send()
        y_across(p).wait_send()

    def lanes(d, whole):
        return slice(None) if whole else (0 if d == 1 else 1)

    def gather_z(c, d, k):
        ref = buf.at[c, lanes(d, k < 3), zk(d, k), :, SECOND]
        return remote(ref, ref, c, SEM_B2 + (0 if d == 1 else 4) + k, z_peer[d])

    def gather_y(c, d, k):
        ref = buf.at[c, lanes(d, k < 1), :, yk(d, k), FIRST]
        return remote(ref, ref, c, SEM_A2 + (0 if d == 1 else 2) + k, y_peer[d])

    def both(make, c, k, action):
        for d in (1, -1):
            getattr(make(c, d, k), action)()

    def rows_of(n):
        return n // 4, pl.ds((n % 4) * 2, 2)

    def rotate(c, half):
        high, low = split_terms(buf[c, half].reshape(ROWS // 2, GROUP))
        if c == GROUPS - 1:
            here = slice(half * (ROWS // 2), (half + 1) * (ROWS // 2))
            terms_out[0, here, :] = high
            terms_out[1, here, :] = low
        part = grad[:, half * (ROWS // 2):(half + 1) * (ROWS // 2)]
        total = jnp.dot(part, high, preferred_element_type=jnp.float32)
        total += jnp.dot(part, low, preferred_element_type=jnp.float32)
        if half == 0:
            rotated[...] = total
        else:
            partial[c] = (rotated[...] + total).T.reshape(2, 2, QUARTER, COLS)

    def rotate_back(c):
        a_high, a_low = split_terms(adjusted[c].reshape(GROUP, COLS).T)

        def body(n, _):
            xn, zn = rows_of(n)
            high, low = split_terms(buf[c, xn, zn].reshape(256, GROUP))
            here = pl.ds(pl.multiple_of(n * 256, 256), 256)
            update[:, here] += back_product(a_high, a_low, high, low)
            return 0
        lax.fori_loop(0, ROWS // 256, body, 0)

    def rs1_copy(c):
        return remote(partial.at[c, :, 1 - core], rs1.at[c], c, SEM_RS1, core_peer)

    def half_rows(i):
        return pl.ds(i * (QUARTER // 2), QUARTER // 2)

    def rs2_copy(c, i):
        return remote(xsend.at[c, half_rows(i)], rs2.at[c, half_rows(i)], c, SEM_RS2 + i, chip_peer)

    def ax_copy(c, i):
        ref = adjusted.at[c, xlo, core, half_rows(i)]
        return remote(ref, ref, c, SEM_AX + i, chip_peer)

    def ac_copy(c, i):
        ref = adjusted.at[c, xlo, core, half_rows(i)]
        return remote(ref, ref, c, SEM_AC + i, core_peer)

    def af_copy(c, i):
        ref = adjusted.at[c, 1 - xlo, core, half_rows(i)]
        return remote(ref, ref, c, SEM_AF + i, core_peer)

    def moments(c, i):
        part = half_rows(i)
        mine = partial[c, xlo, core, part] + rs1[c, xlo, part] + rs2[c, part]
        one = beta_one * first_in[c, part] + (1.0 - beta_one) * mine
        two = beta_two * second_in[c, part] + (1.0 - beta_two) * mine * mine
        first_out[c, part] = one
        second_out[c, part] = two
        adjusted[c, xlo, core, part] = one / correct_one / (jnp.sqrt(two / correct_two) + epsilon)

    def z_step(c, k):
        if k > 0:
            both(gather_z, c, k - 1, "wait_recv")
        both(gather_z, c, k, "start")

    def y_step(c, k):
        if k > 0:
            both(gather_y, c, k - 1, "wait_recv")
        both(gather_y, c, k, "start")

    def arrive(c):
        both(gather_z, c, 3, "wait_recv")
        both(gather_y, c, 1, "wait_recv")
        rotate(c, 0)
        rotate(c, 1)
        rs1_copy(c).start()

    def cross(c):
        rs1_copy(c).wait_recv()
        for i in range(2):
            part = half_rows(i)
            xsend[c, part] = partial[c, 1 - xlo, core, part] + rs1[c, 1 - xlo, part]
            rs2_copy(c, i).start()

    def adjust(c):
        for i in range(2):
            rs2_copy(c, i).wait_recv()
            moments(c, i)
            ax_copy(c, i).start()
            ac_copy(c, i).start()

    def forward(c):
        for i in range(2):
            ax_copy(c, i).wait_recv()
            af_copy(c, i).start()

    def adjusted_ready(c):
        for i in range(2):
            ac_copy(c, i).wait_recv()
            af_copy(c, i).wait_recv()

    def back(c):
        adjusted_ready(c)
        rotate_back(c)

    spread_begin(0)
    spread_y(0)
    spread_begin(1)
    spread_z(0)
    y_across(0).wait_recv()
    z_step(0, 0)
    spread_far(0)
    spread_y(1)
    z_step(1, 0)
    spread_z(1)
    spread_z_ready(0)

    y_step(0, 0)
    z_step(0, 1)
    y_step(1, 0)
    spread_far(1)
    z_step(1, 1)
    y_across(1).wait_recv()
    z_step(0, 2)
    z_step(2, 0)
    y_step(0, 1)
    z_step(0, 3)
    z_step(1, 2)
    spread_z_ready(1)
    y_step(2, 0)
    z_step(2, 1)
    y_step(1, 1)
    z_step(1, 3)
    z_step(3, 0)
    grad_copy.wait()
    prior_copy.wait()
    first_copy.wait()
    second_copy.wait()
    arrive(0)
    z_step(2, 2)
    y_step(3, 0)
    cross(0)
    z_step(3, 1)
    y_step(2, 1)
    arrive(1)
    adjust(0)
    z_step(2, 3)
    cross(1)
    z_step(3, 2)
    y_step(3, 1)
    forward(0)
    arrive(2)
    adjust(1)
    back(0)
    z_step(3, 3)
    cross(2)
    forward(1)
    adjust(2)
    arrive(3)
    back(1)
    cross(3)
    forward(2)
    back(2)
    adjust(3)
    forward(3)
    adjusted_ready(3)
    adjusted_out[...] = adjusted[3]

    dealt.wait_send()
    for p in range(2):
        spread_drain(p)

    for c in range(GROUPS):
        for k in range(4):
            both(gather_z, c, k, "wait_send")
        for k in range(2):
            both(gather_y, c, k, "wait_send")
        rs1_copy(c).wait_send()
        for copy in (rs2_copy, ax_copy, ac_copy, af_copy):
            for i in range(2):
                copy(c, i).wait_send()


def finish_kernel(first_in, second_in, update, terms, adjusted, first_out, second_out, update_out, result, sem):
    copies = [pltpu.make_async_copy(first_in, first_out, sem.at[ROWS // 256]),
              pltpu.make_async_copy(second_in, second_out, sem.at[ROWS // 256 + 1])]
    for copy in copies:
        copy.start()
    a_high, a_low = split_terms(adjusted[...].reshape(GROUP, COLS).T)
    for n in range(ROWS // 256):
        here = slice(n * 256, (n + 1) * 256)
        result[:, here] = update[:, here] + back_product(a_high, a_low, terms[0, here, :], terms[1, here, :])
        copies.append(pltpu.make_async_copy(result.at[:, here], update_out.at[:, here], sem.at[n]))
        copies[-1].start()
    for copy in copies:
        copy.wait()


def step(gradient, eigenbasis, first_moment, second_moment, prior_update, group_ids):
    pieces = eigenbasis.reshape(SPREAD, PIECE, 128)
    vmem = pl.BlockSpec(memory_space=pltpu.VMEM)
    hbm = pl.BlockSpec(memory_space=pl.ANY)
    block = (GROUPS, QUARTER, COLS)
    passed = pl.pallas_call(
        kernel,
        out_shape=(
            jax.ShapeDtypeStruct(block, jnp.float32),
            jax.ShapeDtypeStruct(block, jnp.float32),
            jax.ShapeDtypeStruct((COLS, ROWS), jnp.float32),
            jax.ShapeDtypeStruct((2, ROWS, GROUP), jnp.bfloat16),
            jax.ShapeDtypeStruct((2, 2, QUARTER, COLS), jnp.float32),
        ),
        in_specs=[pl.BlockSpec(memory_space=pltpu.SMEM), hbm, hbm, hbm, hbm, hbm],
        out_specs=(vmem,) * 5,
        scratch_shapes=[
            pltpu.VMEM((SPREAD, PIECE, 128), jnp.float32),
            pltpu.VMEM((GROUPS, NX, NZ, NY, PIECE, GROUP), jnp.float32),
            pltpu.VMEM((COLS, ROWS), jnp.bfloat16),
            pltpu.VMEM((COLS, GROUP), jnp.float32),
            pltpu.VMEM((GROUPS, 2, 2, QUARTER, COLS), jnp.float32),
            pltpu.VMEM((GROUPS, 2, QUARTER, COLS), jnp.float32),
            pltpu.VMEM(block, jnp.float32),
            pltpu.VMEM(block, jnp.float32),
            pltpu.VMEM((GROUPS, 2, 2, QUARTER, COLS), jnp.float32),
            pltpu.SemaphoreType.DMA((GROUPS, SEMS)),
            pltpu.SemaphoreType.DMA((GROUPS, SEMS)),
            pltpu.SemaphoreType.DMA((5,)),
            pltpu.SemaphoreType.DMA,
            pltpu.SemaphoreType.DMA,
            pltpu.SemaphoreType.DMA((2, 20)),
            pltpu.SemaphoreType.DMA((2, 20)),
            pltpu.VMEM(block, jnp.float32),
            pltpu.VMEM(block, jnp.float32),
            pltpu.SemaphoreType.REGULAR((2,)),
        ],
        compiler_params=pltpu.CompilerParams(
            collective_id=0, has_side_effects=True, vmem_limit_bytes=42 * 1024 * 1024),
        cost_estimate=pl.CostEstimate(flops=9_400_000_000, bytes_accessed=14_000_000, transcendentals=0),
    )(group_ids, pieces, first_moment, second_moment, gradient.T, prior_update.T)
    first_out, second_out, update = pl.pallas_call(
        finish_kernel,
        out_shape=(
            jax.ShapeDtypeStruct(block, jnp.float32),
            jax.ShapeDtypeStruct(block, jnp.float32),
            jax.ShapeDtypeStruct((COLS, ROWS), jnp.float32),
        ),
        in_specs=[vmem] * 5,
        out_specs=(hbm,) * 3,
        scratch_shapes=[pltpu.VMEM((COLS, ROWS), jnp.float32), pltpu.SemaphoreType.DMA((ROWS // 256 + 2,))],
        compiler_params=pltpu.CompilerParams(vmem_limit_bytes=24 * 1024 * 1024),
        cost_estimate=pl.CostEstimate(flops=1_400_000_000, bytes_accessed=5_000_000, transcendentals=0),
    )(*passed)
    return first_out, second_out, update.T


def solution(mesh):
    split = P("rows", "cols")
    moment = P(None, "rows", "cols")
    return jax.shard_map(
        step, mesh=mesh,
        in_specs=(split, split, moment, moment, split, P(None)),
        out_specs=(moment, moment, split),
        check_vma=False,
    )
```

time: 139 us -> 123 us (0.88)
  Pallas kernels: 128 us -> 117 us
  local copies, waits for them, and re-layouts: 9.84 us -> 5.45 us
    pallas_call x1, Pallas kernels: 128 us -> 114 us  [step(): pl.pallas_call(kernel, out_shape=(jax.ShapeDtypeStruct(block, jnp.float32...]
    unnamed x11 -> x10, local copies, waits for them, and re-layouts: 9.84 us -> 5.45 us
    pallas_call x0 -> x1, Pallas kernels: none -> 2.91 us  [step(): pl.pallas_call(finish_kernel, out_shape=(jax.ShapeDtypeStruct(block, jnp....]
where the time goes in v3:
time: 123 us
  Pallas kernels  117 us (95%)
  local copies, waits for them, and re-layouts  5.45 us (4%)
    pallas_call x1, Pallas kernels, step(): pl.pallas_call(kernel, out_shape=(jax.ShapeDtypeStruct(block, jnp.float32...  114 us
    unnamed x10, local copies, waits for them, and re-layouts  5.45 us
    pallas_call x1, Pallas kernels, step(): pl.pallas_call(finish_kernel, out_shape=(jax.ShapeDtypeStruct(block, jnp....  2.91 us

profile of v3, /device:TPU:1, one launch (start us, length us, event | category | flops | bytes accessed | tf_op | source)
XLA Modules:
  0.0 123.2 jit_solution(993325340767036298)
XLA Ops:
  0.6 0.0 copy-start
  0.6 1.5 %copy-done = bf16[2048,448]{0,1:T(8,128)(2,1)S(1)} copy-done((bf16[2048,448]{0,1:T(8,128)(2,1)S(1)}, bf16[2048,448]{0,1:T(8,128)(2,1)}, u32[]{:S(2)}) %copy-start) | copy-done | bytes 1835032
  2.1 0.0 copy-start.1
  2.1 1.2 copy-done.1
  3.4 0.0 copy-start.2
  3.4 1.0 copy-done.2
  4.4 0.0 copy-start.3
  4.4 1.0 copy-done.3
  5.4 0.0 copy-start.4
  5.4 0.7 copy-done.4
  6.1 114.2 %shard_map.85 = (f32[4,64,448]{2,1,0:T(8,128)S(1)}, f32[4,64,448]{2,1,0:T(8,128)S(1)}, f32[448,2048]{1,0:T(8,128)S(1)}, bf16[2,2048,256]{2,1,0:T(8,128)(2,1)S(1)}, f32[2,2,64,448]{3,2,1,0:T(8,128)S(1)}) custom-call(s32[4]{0:T(128)S(1)} %copy-done.4, f32[64,32,128]{2,1,0:T(8,128)S(1)} %bitcast.5, f32[4,64,448]{2,1,0:T(8,128)S(1)} %copy-done.2, ...), custom_call_target="tpu_custom_call" | custom-call | flops 9400000512 | bytes 14000000 | tf_op jit(solution)/shard_map/pallas_call | solution.py:425
  120.3 2.9 %shard_map.86 = (f32[4,64,448]{2,1,0:T(8,128)}, f32[4,64,448]{2,1,0:T(8,128)}, f32[448,2048]{1,0:T(8,128)}) custom-call(f32[4,64,448]{2,1,0:T(8,128)S(1)} %get-tuple-element.11.first_in, f32[4,64,448]{2,1,0:T(8,128)S(1)} %get-tuple-element.12.second_in, f32[448,2048]{1,0:T(8,128)S(1)} %get-tuple-element.13.update, ...), custom_call_target="tpu_custom_call" | custom-call | flops 1400000000 | bytes 5000000 | tf_op jit(solution)/shard_map/pallas_call | solution.py:461
Async XLA Ops:
  0.6 1.5 %copy-start = (bf16[2048,448]{0,1:T(8,128)(2,1)S(1)}, bf16[2048,448]{0,1:T(8,128)(2,1)}, u32[]{:S(2)}) copy-start(bf16[2048,448]{0,1:T(8,128)(2,1)} %param.6) | copy-start | bytes 5505028
  2.1 1.2 copy-start.1
  3.4 1.0 copy-start.2
  4.4 1.0 copy-start.3
  5.4 0.7 copy-start.4

commit v4 on v3

--- a/solution.py
+++ b/solution.py
@@ -27,8 +27,8 @@
 FIRST, SECOND = pl.ds(0, 16), pl.ds(16, 16)
 
 SEM_A2 = 0
-SEM_B2 = SEM_A2 + 4
-SEM_RS1 = SEM_B2 + 8
+SEM_B2 = SEM_A2 + 6
+SEM_RS1 = SEM_B2 + 10
 SEM_RS2 = SEM_RS1 + 1
 SEM_AX = SEM_RS2 + 2
 SEM_AC = SEM_AX + 2
@@ -50,10 +50,10 @@
 
 
 def kernel(ids, basis_hbm, first_hbm, second_hbm, grad_hbm, prior_hbm,
-           first_out, second_out, update, terms_out, adjusted_out,
+           first_out, second_out, adjusted_out, update_out, terms_out,
            pieces, buf, grad, rotated, partial, rs1, xsend, rs2, adjusted,
            send_sem, recv_sem, local_sem, deal_send, deal_recv,
-           spread_send, spread_recv, first_in, second_in, met):
+           spread_send, spread_recv, first_in, second_in, met, update, terms):
     cols = lax.axis_index("cols")
     rows = lax.axis_index("rows")
     xh = cols // (NZ * NY)
@@ -66,12 +66,15 @@
     def at(xh_, z_, y_):
         return (xh_ * NZ + z_) * NY + y_
 
+    own, other = xh, 1 - xh
     x_peer = (at(1 - xh, z, y), rows)
     z_peer = {d: (at(xh, (z + d * sign + NZ) % NZ, y), rows) for d in (1, -1)}
     y_peer = {d: (at(xh, z, (y + d * sign + NY) % NY), rows) for d in (1, -1)}
     core_peer = (cols, xlo * 2 + 1 - core)
     chip_peer = (cols, (1 - xlo) * 2 + core)
 
+    update_copy = pltpu.make_async_copy(update, update_out, local_sem.at[5])
+    terms_copy = pltpu.make_async_copy(terms, terms_out, local_sem.at[6])
     grad_copy = pltpu.make_async_copy(grad_hbm, grad, local_sem.at[0])
     prior_copy = pltpu.make_async_copy(prior_hbm, update, local_sem.at[1])
     first_copy = pltpu.make_async_copy(first_hbm, first_in, local_sem.at[3])
@@ -209,17 +212,34 @@
     def lanes(d, whole):
         return slice(None) if whole else (0 if d == 1 else 1)
 
+    def begin_z(c, d, part):
+        ref = buf.at[c, own if part == 0 else other, z, :, SECOND]
+        return remote(ref, ref, c, SEM_B2 + (0 if d == 1 else 5) + part, z_peer[d])
+
+    def begin_y(c, d, part):
+        ref = buf.at[c, own if part == 0 else other, :, y, FIRST]
+        return remote(ref, ref, c, SEM_A2 + (0 if d == 1 else 3) + part, y_peer[d])
+
     def gather_z(c, d, k):
         ref = buf.at[c, lanes(d, k < 3), zk(d, k), :, SECOND]
-        return remote(ref, ref, c, SEM_B2 + (0 if d == 1 else 4) + k, z_peer[d])
+        return remote(ref, ref, c, SEM_B2 + (0 if d == 1 else 5) + k + 1, z_peer[d])
 
     def gather_y(c, d, k):
-        ref = buf.at[c, lanes(d, k < 1), :, yk(d, k), FIRST]
-        return remote(ref, ref, c, SEM_A2 + (0 if d == 1 else 2) + k, y_peer[d])
+        ref = buf.at[c, lanes(d, False), :, yk(d, k), FIRST]
+        return remote(ref, ref, c, SEM_A2 + (0 if d == 1 else 3) + k + 1, y_peer[d])
 
     def both(make, c, k, action):
         for d in (1, -1):
-            getattr(make(c, d, k), action)()
+            if k == 0:
+                begin = begin_z if make is gather_z else begin_y
+                for part in range(2):
+                    getattr(begin(c, d, part), action)()
+            else:
+                getattr(make(c, d, k), action)()
+
+    def begin(make, c, part):
+        for d in (1, -1):
+            make(c, d, part).start()
 
     def rows_of(n):
         return n // 4, pl.ds((n % 4) * 2, 2)
@@ -228,8 +248,8 @@
         high, low = split_terms(buf[c, half].reshape(ROWS // 2, GROUP))
         if c == GROUPS - 1:
             here = slice(half * (ROWS // 2), (half + 1) * (ROWS // 2))
-            terms_out[0, here, :] = high
-            terms_out[1, here, :] = low
+            terms[0, here, :] = high
+            terms[1, here, :] = low
         part = grad[:, half * (ROWS // 2):(half + 1) * (ROWS // 2)]
         total = jnp.dot(part, high, preferred_element_type=jnp.float32)
         total += jnp.dot(part, low, preferred_element_type=jnp.float32)
@@ -326,19 +346,23 @@
 
     spread_begin(0)
     spread_y(0)
+    begin(begin_z, 0, 0)
+    spread_z(0)
     spread_begin(1)
-    spread_z(0)
+    begin(begin_z, 1, 0)
+    spread_far(0)
+    begin(begin_y, 0, 0)
     y_across(0).wait_recv()
-    z_step(0, 0)
-    spread_far(0)
+    begin(begin_z, 0, 1)
+    begin(begin_y, 1, 0)
+    begin(begin_z, 1, 1)
     spread_y(1)
-    z_step(1, 0)
+    spread_z_ready(0)
+    begin(begin_y, 0, 1)
+    begin(begin_y, 1, 1)
+
     spread_z(1)
-    spread_z_ready(0)
-
-    y_step(0, 0)
     z_step(0, 1)
-    y_step(1, 0)
     spread_far(1)
     z_step(1, 1)
     y_across(1).wait_recv()
@@ -351,6 +375,7 @@
     y_step(2, 0)
     z_step(2, 1)
     y_step(1, 1)
+    y_step(3, 0)
     z_step(1, 3)
     z_step(3, 0)
     grad_copy.wait()
@@ -359,33 +384,36 @@
     second_copy.wait()
     arrive(0)
     z_step(2, 2)
-    y_step(3, 0)
     cross(0)
     z_step(3, 1)
     y_step(2, 1)
     arrive(1)
     adjust(0)
     z_step(2, 3)
+    y_step(3, 1)
     cross(1)
     z_step(3, 2)
-    y_step(3, 1)
     forward(0)
     arrive(2)
+    z_step(3, 3)
     adjust(1)
+    cross(2)
     back(0)
-    z_step(3, 3)
-    cross(2)
     forward(1)
+    arrive(3)
+    terms_copy.start()
     adjust(2)
-    arrive(3)
+    cross(3)
     back(1)
-    cross(3)
     forward(2)
+    adjust(3)
     back(2)
-    adjust(3)
+    update_copy.start()
     forward(3)
     adjusted_ready(3)
     adjusted_out[...] = adjusted[3]
+    terms_copy.wait()
+    update_copy.wait()
 
     dealt.wait_send()
     for p in range(2):
@@ -402,7 +430,7 @@
                 copy(c, i).wait_send()
 
 
-def finish_kernel(first_in, second_in, update, terms, adjusted, first_out, second_out, update_out, result, sem):
+def finish_kernel(first_in, second_in, adjusted, update, terms, first_out, second_out, update_out, result, sem):
     copies = [pltpu.make_async_copy(first_in, first_out, sem.at[ROWS // 256]),
               pltpu.make_async_copy(second_in, second_out, sem.at[ROWS // 256 + 1])]
     for copy in copies:
@@ -427,12 +455,12 @@
         out_shape=(
             jax.ShapeDtypeStruct(block, jnp.float32),
             jax.ShapeDtypeStruct(block, jnp.float32),
+            jax.ShapeDtypeStruct((2, 2, QUARTER, COLS), jnp.float32),
             jax.ShapeDtypeStruct((COLS, ROWS), jnp.float32),
             jax.ShapeDtypeStruct((2, ROWS, GROUP), jnp.bfloat16),
-            jax.ShapeDtypeStruct((2, 2, QUARTER, COLS), jnp.float32),
         ),
         in_specs=[pl.BlockSpec(memory_space=pltpu.SMEM), hbm, hbm, hbm, hbm, hbm],
-        out_specs=(vmem,) * 5,
+        out_specs=(vmem, vmem, vmem, hbm, hbm),
         scratch_shapes=[
             pltpu.VMEM((SPREAD, PIECE, 128), jnp.float32),
             pltpu.VMEM((GROUPS, NX, NZ, NY, PIECE, GROUP), jnp.float32),
@@ -445,7 +473,7 @@
             pltpu.VMEM((GROUPS, 2, 2, QUARTER, COLS), jnp.float32),
             pltpu.SemaphoreType.DMA((GROUPS, SEMS)),
             pltpu.SemaphoreType.DMA((GROUPS, SEMS)),
-            pltpu.SemaphoreType.DMA((5,)),
+            pltpu.SemaphoreType.DMA((7,)),
             pltpu.SemaphoreType.DMA,
             pltpu.SemaphoreType.DMA,
             pltpu.SemaphoreType.DMA((2, 20)),
@@ -453,9 +481,11 @@
             pltpu.VMEM(block, jnp.float32),
             pltpu.VMEM(block, jnp.float32),
             pltpu.SemaphoreType.REGULAR((2,)),
+            pltpu.VMEM((COLS, ROWS), jnp.float32),
+            pltpu.VMEM((2, ROWS, GROUP), jnp.bfloat16),
         ],
         compiler_params=pltpu.CompilerParams(
-            collective_id=0, has_side_effects=True, vmem_limit_bytes=42 * 1024 * 1024),
+            collective_id=0, has_side_effects=True, vmem_limit_bytes=52 * 1024 * 1024),
         cost_estimate=pl.CostEstimate(flops=9_400_000_000, bytes_accessed=14_000_000, transcendentals=0),
     )(group_ids, pieces, first_moment, second_moment, gradient.T, prior_update.T)
     first_out, second_out, update = pl.pallas_call(

time: 123 us -> 118 us (0.959)
  Pallas kernels: 117 us -> 113 us
    pallas_call x1, Pallas kernels: 114 us -> 110 us  [step(): pl.pallas_call(kernel, out_shape=(jax.ShapeDtypeStruct(block, jnp.float32...]
    unnamed x10 -> x6, local copies, waits for them, and re-layouts: 5.45 us -> 4.27 us
where the time goes in v4:
time: 118 us
  Pallas kernels  113 us (96%)
  local copies, waits for them, and re-layouts  4.27 us (4%)
    pallas_call x1, Pallas kernels, step(): pl.pallas_call(kernel, out_shape=(jax.ShapeDtypeStruct(block, jnp.float32...  110 us
    unnamed x6, local copies, waits for them, and re-layouts  4.27 us
    pallas_call x1, Pallas kernels, step(): pl.pallas_call(finish_kernel, out_shape=(jax.ShapeDtypeStruct(block, jnp....  2.85 us

profile of v4, /device:TPU:1, one launch (start us, length us, event | category | flops | bytes accessed | tf_op | source)
XLA Modules:
  0.0 118.0 jit_solution(17050168440628008663)
XLA Ops:
  0.6 0.0 copy-start.2
  0.6 0.6 copy-done.2
  1.3 110.2 %shard_map.85 = (f32[4,64,448]{2,1,0:T(8,128)S(1)}, f32[4,64,448]{2,1,0:T(8,128)S(1)}, f32[2,2,64,448]{3,2,1,0:T(8,128)S(1)}, f32[448,2048]{1,0:T(8,128)}, bf16[2,2048,256]{2,1,0:T(8,128)(2,1)}) custom-call(s32[4]{0:T(128)S(1)} %copy-done.2, f32[64,32,128]{2,1,0:T(8,128)} %bitcast.7, f32[4,64,448]{2,1,0:T(8,128)} %first_hbm.1, f32[4,64,448]{2,1,0:T(8,128)} %second_hbm.1, ...), custom_call_target="tpu_custom_call" | custom-call | flops 9400000512 | bytes 14000000 | tf_op jit(solution)/shard_map/pallas_call | solution.py:453
  111.5 0.0 copy-start
  111.5 2.0 %copy-done = f32[448,2048]{1,0:T(8,128)S(1)} copy-done((f32[448,2048]{1,0:T(8,128)S(1)}, f32[448,2048]{1,0:T(8,128)}, u32[]{:S(2)}) %copy-start) | copy-done | bytes 3670040
  113.5 0.0 copy-start.1
  113.5 1.6 %copy-done.1 = bf16[2,2048,256]{2,1,0:T(8,128)(2,1)S(1)} copy-done((bf16[2,2048,256]{2,1,0:T(8,128)(2,1)S(1)}, bf16[2,2048,256]{2,1,0:T(8,128)(2,1)}, u32[]{:S(2)}) %copy-start.1) | copy-done | bytes 2097176
  115.1 2.9 %shard_map.86 = (f32[4,64,448]{2,1,0:T(8,128)}, f32[4,64,448]{2,1,0:T(8,128)}, f32[448,2048]{1,0:T(8,128)}) custom-call(f32[4,64,448]{2,1,0:T(8,128)S(1)} %get-tuple-element.11.first_in, f32[4,64,448]{2,1,0:T(8,128)S(1)} %get-tuple-element.12.second_in, f32[2,2,64,448]{3,2,1,0:T(8,128)S(1)} %get-tuple-element.13.adjusted, f32[448,2048]{1,0:T(8,128)S(1)} %copy-done, ...), custom_call_target="tpu_custom_call" | custom-call | flops 1400000000 | bytes 5000000 | tf_op jit(solution)/shard_map/pallas_call | solution.py:491
Async XLA Ops:
  0.6 0.7 copy-start.2
  111.5 2.0 %copy-start = (f32[448,2048]{1,0:T(8,128)S(1)}, f32[448,2048]{1,0:T(8,128)}, u32[]{:S(2)}) copy-start(f32[448,2048]{1,0:T(8,128)} %get-tuple-element.14.update) | copy-start | bytes 11010052
  113.5 1.6 %copy-start.1 = (bf16[2,2048,256]{2,1,0:T(8,128)(2,1)S(1)}, bf16[2,2048,256]{2,1,0:T(8,128)(2,1)}, u32[]{:S(2)}) copy-start(bf16[2,2048,256]{2,1,0:T(8,128)(2,1)} %get-tuple-element.15.terms) | copy-start | bytes 6291460

commit v5 on v4

--- a/solution.py
+++ b/solution.py
@@ -24,7 +24,12 @@
 correct_two = 1.0 - 0.95**10
 epsilon = 1e-08
 
-FIRST, SECOND = pl.ds(0, 16), pl.ds(16, 16)
+BATCHES = ((0, 2, 16), (2, 1, 24), (3, 1, 16))
+SLOTS = [pl.ds(begin, count) for begin, count, _ in BATCHES]
+FIRST = [pl.ds(0, cut) for _, _, cut in BATCHES]
+SECOND = [pl.ds(cut, PIECE - cut) for _, _, cut in BATCHES]
+SHARED = [(pl.ds(0, 8), pl.ds(8, cut - 8)) for _, _, cut in BATCHES]
+BATCH_OF = (0, 0, 1, 2)
 
 SEM_A2 = 0
 SEM_B2 = SEM_A2 + 6
@@ -144,7 +149,7 @@
             device_id=peer, device_id_type=MESH)
 
     def z_block(p, j):
-        return buf.at[pl.ds(2 * p, 2), xh, zk(1, -j), y, FIRST]
+        return buf.at[SLOTS[p], xh, zk(1, -j), y, FIRST[p]]
 
     def z_near(p, j):
         return spread(z_block(p, 0), p, 2 + j if j < 0 else 1 + j, (at(xh, zk(1, -j), y), rows))
@@ -153,17 +158,17 @@
         return spread(z_block(p, -2 * d), p, 4 if d == 1 else 5, (at(xh, zk(1, -d), y), rows))
 
     def z_fourth(p, d):
-        src = buf.at[2 * p + (0 if d == 1 else 1), xh, zk(1, 2 * d), y, FIRST]
+        src = buf.at[SLOTS[p], xh, zk(1, 2 * d), y, SHARED[p][0 if d == 1 else 1]]
         return spread(src, p, 6 if d == 1 else 7, (at(xh, zk(1, -2 * d), y), rows))
 
     def z_across(p, j):
         return spread(z_block(p, j), p, 8 + j % NZ, x_peer)
 
     def y_near(p, j):
-        return spread(buf.at[pl.ds(2 * p, 2), xh, z, y, SECOND], p, 15 + j, (at(xh, z, (y + j) % NY), rows))
+        return spread(buf.at[SLOTS[p], xh, z, y, SECOND[p]], p, 15 + j, (at(xh, z, (y + j) % NY), rows))
 
     def y_across(p):
-        return spread(buf.at[pl.ds(2 * p, 2), xh, z, :, SECOND], p, 19, x_peer)
+        return spread(buf.at[SLOTS[p], xh, z, :, SECOND[p]], p, 19, x_peer)
 
     def spread_begin(p):
         for j in (1, 2, 3):
@@ -213,19 +218,19 @@
         return slice(None) if whole else (0 if d == 1 else 1)
 
     def begin_z(c, d, part):
-        ref = buf.at[c, own if part == 0 else other, z, :, SECOND]
+        ref = buf.at[c, own if part == 0 else other, z, :, SECOND[BATCH_OF[c]]]
         return remote(ref, ref, c, SEM_B2 + (0 if d == 1 else 5) + part, z_peer[d])
 
     def begin_y(c, d, part):
-        ref = buf.at[c, own if part == 0 else other, :, y, FIRST]
+        ref = buf.at[c, own if part == 0 else other, :, y, FIRST[BATCH_OF[c]]]
         return remote(ref, ref, c, SEM_A2 + (0 if d == 1 else 3) + part, y_peer[d])
 
     def gather_z(c, d, k):
-        ref = buf.at[c, lanes(d, k < 3), zk(d, k), :, SECOND]
+        ref = buf.at[c, lanes(d, k < 3), zk(d, k), :, SECOND[BATCH_OF[c]]]
         return remote(ref, ref, c, SEM_B2 + (0 if d == 1 else 5) + k + 1, z_peer[d])
 
     def gather_y(c, d, k):
-        ref = buf.at[c, lanes(d, False), :, yk(d, k), FIRST]
+        ref = buf.at[c, lanes(d, False), :, yk(d, k), FIRST[BATCH_OF[c]]]
         return remote(ref, ref, c, SEM_A2 + (0 if d == 1 else 3) + k + 1, y_peer[d])
 
     def both(make, c, k, action):
@@ -356,27 +361,33 @@
     begin(begin_z, 0, 1)
     begin(begin_y, 1, 0)
     begin(begin_z, 1, 1)
+    spread_begin(2)
     spread_y(1)
     spread_z_ready(0)
     begin(begin_y, 0, 1)
     begin(begin_y, 1, 1)
 
+    spread_y(2)
     spread_z(1)
     z_step(0, 1)
+    spread_z(2)
     spread_far(1)
     z_step(1, 1)
     y_across(1).wait_recv()
     z_step(0, 2)
     z_step(2, 0)
     y_step(0, 1)
+    spread_far(2)
     z_step(0, 3)
     z_step(1, 2)
     spread_z_ready(1)
     y_step(2, 0)
     z_step(2, 1)
     y_step(1, 1)
+    spread_z_ready(2)
     y_step(3, 0)
     z_step(1, 3)
+    y_across(2).wait_recv()
     z_step(3, 0)
     grad_copy.wait()
     prior_copy.wait()
@@ -416,7 +427,7 @@
     update_copy.wait()
 
     dealt.wait_send()
-    for p in range(2):
+    for p in range(len(BATCHES)):
         spread_drain(p)
 
     for c in range(GROUPS):
@@ -476,8 +487,8 @@
             pltpu.SemaphoreType.DMA((7,)),
             pltpu.SemaphoreType.DMA,
             pltpu.SemaphoreType.DMA,
-            pltpu.SemaphoreType.DMA((2, 20)),
-            pltpu.SemaphoreType.DMA((2, 20)),
+            pltpu.SemaphoreType.DMA((len(BATCHES), 20)),
+            pltpu.SemaphoreType.DMA((len(BATCHES), 20)),
             pltpu.VMEM(block, jnp.float32),
             pltpu.VMEM(block, jnp.float32),
             pltpu.SemaphoreType.REGULAR((2,)),

time: 118 us -> 119 us (level)
  no operation moved by 1% of the time
where the time goes in v5:
time: 119 us; the launch traced here: 118 us
  Pallas kernels  113 us (95%)
  local copies, waits for them, and re-layouts  4.27 us (4%)
    pallas_call x1, Pallas kernels, step(): pl.pallas_call(kernel, out_shape=(jax.ShapeDtypeStruct(block, jnp.float32...  111 us
    unnamed x6, local copies, waits for them, and re-layouts  4.27 us
    pallas_call x1, Pallas kernels, step(): pl.pallas_call(finish_kernel, out_shape=(jax.ShapeDtypeStruct(block, jnp....  2.86 us

profile of v5, /device:TPU:1, one launch (start us, length us, event | category | flops | bytes accessed | tf_op | source)
XLA Modules:
  0.0 118.4 jit_solution(4918654695039474685)
XLA Ops:
  0.6 0.0 copy-start.2
  0.6 0.6 copy-done.2
  1.3 110.6 %shard_map.85 = (f32[4,64,448]{2,1,0:T(8,128)S(1)}, f32[4,64,448]{2,1,0:T(8,128)S(1)}, f32[2,2,64,448]{3,2,1,0:T(8,128)S(1)}, f32[448,2048]{1,0:T(8,128)}, bf16[2,2048,256]{2,1,0:T(8,128)(2,1)}) custom-call(s32[4]{0:T(128)S(1)} %copy-done.2, f32[64,32,128]{2,1,0:T(8,128)} %bitcast.7, f32[4,64,448]{2,1,0:T(8,128)} %first_hbm.1, f32[4,64,448]{2,1,0:T(8,128)} %second_hbm.1, ...), custom_call_target="tpu_custom_call" | custom-call | flops 9400000512 | bytes 14000000 | tf_op jit(solution)/shard_map/pallas_call | solution.py:464
  111.9 0.0 copy-start
  111.9 2.0 %copy-done = f32[448,2048]{1,0:T(8,128)S(1)} copy-done((f32[448,2048]{1,0:T(8,128)S(1)}, f32[448,2048]{1,0:T(8,128)}, u32[]{:S(2)}) %copy-start) | copy-done | bytes 3670040
  113.9 0.0 copy-start.1
  113.9 1.6 %copy-done.1 = bf16[2,2048,256]{2,1,0:T(8,128)(2,1)S(1)} copy-done((bf16[2,2048,256]{2,1,0:T(8,128)(2,1)S(1)}, bf16[2,2048,256]{2,1,0:T(8,128)(2,1)}, u32[]{:S(2)}) %copy-start.1) | copy-done | bytes 2097176
  115.5 2.9 %shard_map.86 = (f32[4,64,448]{2,1,0:T(8,128)}, f32[4,64,448]{2,1,0:T(8,128)}, f32[448,2048]{1,0:T(8,128)}) custom-call(f32[4,64,448]{2,1,0:T(8,128)S(1)} %get-tuple-element.11.first_in, f32[4,64,448]{2,1,0:T(8,128)S(1)} %get-tuple-element.12.second_in, f32[2,2,64,448]{3,2,1,0:T(8,128)S(1)} %get-tuple-element.13.adjusted, f32[448,2048]{1,0:T(8,128)S(1)} %copy-done, ...), custom_call_target="tpu_custom_call" | custom-call | flops 1400000000 | bytes 5000000 | tf_op jit(solution)/shard_map/pallas_call | solution.py:502
Async XLA Ops:
  0.6 0.7 copy-start.2
  111.9 2.0 %copy-start = (f32[448,2048]{1,0:T(8,128)S(1)}, f32[448,2048]{1,0:T(8,128)}, u32[]{:S(2)}) copy-start(f32[448,2048]{1,0:T(8,128)} %get-tuple-element.14.update) | copy-start | bytes 11010052
  113.9 1.6 %copy-start.1 = (bf16[2,2048,256]{2,1,0:T(8,128)(2,1)S(1)}, bf16[2,2048,256]{2,1,0:T(8,128)(2,1)}, u32[]{:S(2)}) copy-start(bf16[2,2048,256]{2,1,0:T(8,128)(2,1)} %get-tuple-element.15.terms) | copy-start | bytes 6291460
